TPU v7x, 32 devices: a whole 2x2x4 slice. The times are simulated.
32 devices in a mesh: freq: 2 (over y), rcv: 4 (over z), src: 4 (over x, core).
Axes of the slice: x: 2, y: 2, z: 4, core: 2. Of those that a mesh axis runs over, the one named last changes fastest.
Arguments:
- traces: float32 [256, 2, 4096], P(('freq', 'src'), None, 'rcv'), parts along dimension 0, may hold values from -6 to 6
- moveout: float32 [2, 64, 16], P(None, 'freq'), parts along dimension 1, may hold values from -0.75 to 0.75
- trace_owner: int32 [8192], P(('freq', 'rcv')), parts along dimension 0, may hold values from 0 to 3, as said below
- trace_group: int32 [8192], P(('freq', 'rcv')), parts along dimension 0, may hold values from 0 to 127
- trace_table: int32 [8192], P(('freq', 'rcv')), parts along dimension 0, may hold values from 0 to 31
- aperture: float32 [2, 16384, 8192], P(None, ('freq', 'rcv'), 'src'), parts along dimension 1, may hold values from -0.046875 to 0.046875
- shaping: float32 [256, 2, 8192], P(('freq', 'src'), None, 'rcv'), parts along dimension 0, may hold values from -0.5 to 0.5
Outputs:
- demultiple: float32 [256, 2, 8192], P(('freq', 'src'), None, 'rcv'), parts along dimension 0
There are 2 independent parts, one for each index of `freq`. A program takes and returns all parts, laid end to end along the dimension named above; each array names one. Nothing has to cross between parts.
Inputs may be any that keep to these rules, and one draw needn't show every extreme that they name: `trace_owner`: among the 1024 traces of each index of rcv (aligned blocks of the array), at most 512 name the same owner, and in every draw some owner is named by exactly 512 traces of every block.
All inputs are finite; a program needn't handle non-finite values.
Results may differ from a plain program's by a relative error of at most 0.0001.
Values sent between devices are 32-bit elements; how exact they have to be, the bound alone decides.
No kernel may reach another device: no remote copies, remote signals or barrier semaphores. Data moves between devices by JAX's collectives and lax.ppermute only.
A program may use at most 128 MiB of HBM per device.

v0:
```python
import jax
import jax.numpy as jnp
from jax import lax
from jax.sharding import PartitionSpec as P

ITERS = 2


def from_root(value, axis, source):
    kept = jnp.where(lax.axis_index(axis) == source, value, 0).astype(value.dtype)
    return lax.psum(kept, axis)


def complex_join(partial_terms):
    return jnp.stack(
        [
            partial_terms[:, 0, 0] - partial_terms[:, 1, 1],
            partial_terms[:, 0, 1] + partial_terms[:, 1, 0],
        ],
        axis=1,
    )


def complex_product(left_side, right_side):
    real_part = left_side[:, 0] * right_side[:, 0] - left_side[:, 1] * right_side[:, 1]
    imag_part = left_side[:, 0] * right_side[:, 1] + left_side[:, 1] * right_side[:, 0]
    return jnp.stack([real_part, imag_part], axis=1)


def bin_matrix(group_code, table_code, moveout, groups, owner_mask):
    group_hot = (group_code[:, None] == jnp.arange(groups)[None, :]).astype(jnp.float32)
    group_hot = group_hot * owner_mask[:, None]
    table_hot = (table_code[:, None] == jnp.arange(moveout.shape[1])[None, :]).astype(jnp.float32)
    weights = jnp.einsum("tk,ckj->tcj", table_hot, moveout, precision=lax.Precision.HIGHEST)
    matrix = group_hot[:, None, :, None] * weights[:, :, None, :]
    return matrix.reshape(matrix.shape[0], 2, groups * moveout.shape[2])


def interpolate(values, matrix):
    return complex_join(
        jnp.einsum("sct,tdb->scdb", values, matrix, precision=lax.Precision.HIGHEST)
    )


def to_columns(panel_now):
    shots_all = lax.all_gather(panel_now, "src", axis=0, tiled=True)
    fold_count = lax.axis_size("rcv") // lax.axis_size("src")
    first_root = fold_count * lax.axis_index("src")
    pieces = [from_root(shots_all, "rcv", first_root + offset) for offset in range(fold_count)]
    return jnp.concatenate(pieces, axis=2)


def multiply(columns, aperture):
    return lax.psum_scatter(
        complex_join(
            jnp.einsum("sck,dik->scdi", columns, aperture, precision=lax.Precision.HIGHEST)
        ),
        "src",
        scatter_dimension=0,
        tiled=True,
    )


def per_device(traces, moveout, trace_owner, trace_group, trace_table, aperture, shaping):
    groups = aperture.shape[1] // moveout.shape[2]

    def one_owner(owner_index):
        owner_mask = (trace_owner == owner_index).astype(jnp.float32)
        matrix = bin_matrix(trace_group, trace_table, moveout, groups, owner_mask)
        return interpolate(traces, matrix)

    binned = lax.psum_scatter(
        lax.map(one_owner, jnp.arange(1 * lax.axis_size("rcv"), dtype=jnp.int32)),
        "rcv",
        scatter_dimension=0,
        tiled=True,
    )[0]
    panel_now = binned
    for sweep_index in range(ITERS):
        multiples = multiply(to_columns(panel_now), aperture)
        panel_now = binned - complex_product(shaping, multiples)
    return panel_now


def solution(mesh):
    in_specs = (
        P(("freq", "src"), None, "rcv"),
        P(None, "freq", None),
        P(("freq", "rcv")),
        P(("freq", "rcv")),
        P(("freq", "rcv")),
        P(None, ("freq", "rcv"), "src"),
        P(("freq", "src"), None, "rcv"),
    )
    out_specs = P(("freq", "src"), None, "rcv")
    return jax.shard_map(
        per_device, mesh=mesh, in_specs=in_specs, out_specs=out_specs, check_vma=False
    )
```

profile of v0, /device:TPU:0, one launch (start us, length us, event | category | flops | bytes accessed | tf_op | source)
XLA Modules:
  0.0 582.9 jit_solution(2520688945853668558)
XLA Ops:
  6.5 1.0 copy.18
  7.6 160.8 %while.10 = (s32[]{:T(128)}, f32[4,32,2,2048]{3,1,2,0:T(8,128)}, s32[1024]{0:T(1024)}, s32[4]{0:T(128)S(1)}, s32[1024]{0:T(1024)}, /*index=5*/s32[1024]{0:T(1024...) while((s32[]{:T(128)}, f32[4,32,2,2048]{3,1,2,0:T(8,128)}, s32[1024]{0:T(1024)}, s32[4]{0:T(128)S(1)}, ...), condition=%wide.region_1.2_spmd, body=%wide.region_0.1_spmd.sunk | while | flops 3238561792 | bytes 55632548 | solution.py:73
  7.6 0.6 dynamic_slice.5
  8.2 1.3 compare_convert_fusion.2
  9.5 0.7 fusion.38
  10.3 4.3 mul.92
  14.8 12.2 %bitcast_multiply_fusion.2 = f32[1024,2,2048]{0,2,1:T(8,128)} fusion(f32[1024,2,16]{0,2,1:T(8,128)S(1)} %bitcast.96, f32[1024,2048]{0,1:T(8,128)} %bitcast.95), kind=kLoop, calls=%fused_computation.2.clone.1 | loop fusion | flops 4194304 | bytes 25296896 | tf_op jit(solution)/shard_map/while/body/eval_jaxpr/mul | solution.py:35
  27.1 19.8 %fusion.39 = f32[32,2,2,2048]{3,0,1,2:T(8,128)S(1)} fusion(f32[1024,2,2048]{0,2,1:T(8,128)} %bitcast_multiply_fusion.2, f32[32,2,1024]{2,0,1:T(8,128)S(1)} %get-tuple-element.164), kind=kOutput, calls=%fused_computation.3.clone.1 | convolution fusion | flops 3221225472 | bytes 18087936 | tf_op jit(solution)/shard_map/while/body/eval_jaxpr/sct,tdb->scdb/dot_general | solution.py:41
  46.9 0.9 fusion.42
  47.8 0.6 dynamic_slice.5
  48.4 1.3 compare_convert_fusion.2
  49.7 0.7 fusion.38
  50.5 4.3 mul.92
  55.0 12.2 %bitcast_multiply_fusion.2 = f32[1024,2,2048]{0,2,1:T(8,128)} fusion(f32[1024,2,16]{0,2,1:T(8,128)S(1)} %bitcast.96, f32[1024,2048]{0,1:T(8,128)} %bitcast.95), kind=kLoop, calls=%fused_computation.2.clone.1 | loop fusion | flops 4194304 | bytes 25296896 | tf_op jit(solution)/shard_map/while/body/eval_jaxpr/mul | solution.py:35
  67.3 19.8 %fusion.39 = f32[32,2,2,2048]{3,0,1,2:T(8,128)S(1)} fusion(f32[1024,2,2048]{0,2,1:T(8,128)} %bitcast_multiply_fusion.2, f32[32,2,1024]{2,0,1:T(8,128)S(1)} %get-tuple-element.164), kind=kOutput, calls=%fused_computation.3.clone.1 | convolution fusion | flops 3221225472 | bytes 18087936 | tf_op jit(solution)/shard_map/while/body/eval_jaxpr/sct,tdb->scdb/dot_general | solution.py:41
  87.1 0.9 fusion.42
  88.0 0.6 dynamic_slice.5
  88.6 1.3 compare_convert_fusion.2
  89.9 0.7 fusion.38
  90.7 4.3 mul.92
  95.2 12.2 %bitcast_multiply_fusion.2 = f32[1024,2,2048]{0,2,1:T(8,128)} fusion(f32[1024,2,16]{0,2,1:T(8,128)S(1)} %bitcast.96, f32[1024,2048]{0,1:T(8,128)} %bitcast.95), kind=kLoop, calls=%fused_computation.2.clone.1 | loop fusion | flops 4194304 | bytes 25296896 | tf_op jit(solution)/shard_map/while/body/eval_jaxpr/mul | solution.py:35
  107.5 19.8 %fusion.39 = f32[32,2,2,2048]{3,0,1,2:T(8,128)S(1)} fusion(f32[1024,2,2048]{0,2,1:T(8,128)} %bitcast_multiply_fusion.2, f32[32,2,1024]{2,0,1:T(8,128)S(1)} %get-tuple-element.164), kind=kOutput, calls=%fused_computation.3.clone.1 | convolution fusion | flops 3221225472 | bytes 18087936 | tf_op jit(solution)/shard_map/while/body/eval_jaxpr/sct,tdb->scdb/dot_general | solution.py:41
  127.3 0.9 fusion.42
  128.2 0.6 dynamic_slice.5
  128.8 1.3 compare_convert_fusion.2
  130.1 0.7 fusion.38
  130.9 4.3 mul.92
  135.4 12.2 %bitcast_multiply_fusion.2 = f32[1024,2,2048]{0,2,1:T(8,128)} fusion(f32[1024,2,16]{0,2,1:T(8,128)S(1)} %bitcast.96, f32[1024,2048]{0,1:T(8,128)} %bitcast.95), kind=kLoop, calls=%fused_computation.2.clone.1 | loop fusion | flops 4194304 | bytes 25296896 | tf_op jit(solution)/shard_map/while/body/eval_jaxpr/mul | solution.py:35
  147.6 19.8 %fusion.39 = f32[32,2,2,2048]{3,0,1,2:T(8,128)S(1)} fusion(f32[1024,2,2048]{0,2,1:T(8,128)} %bitcast_multiply_fusion.2, f32[32,2,1024]{2,0,1:T(8,128)S(1)} %get-tuple-element.164), kind=kOutput, calls=%fused_computation.3.clone.1 | convolution fusion | flops 3221225472 | bytes 18087936 | tf_op jit(solution)/shard_map/while/body/eval_jaxpr/sct,tdb->scdb/dot_general | solution.py:41
  167.5 0.9 fusion.42
  168.5 46.7 %reduce-scatter.4.cloned.1.call-done = f32[1,32,2,2048]{3,1,2,0:T(8,128)} async-done(((f32[4,32,2,2048]{3,1,2,0:T(8,128)}), f32[1,32,2,2048]{3,1,2,0:T(8,128)}) %reduce-scatter.4.cloned.1.call-update) | async-done | bytes 524304 | tf_op jit(solution)/shard_map/reduce_scatter | solution.py:72
  215.2 23.5 %all-gather.6.cloned.1.call-done = f32[1,128,2,2048]{3,1,2,0:T(8,128)} async-done(((f32[1,32,2,2048]{3,1,2,0:T(8,128)}), f32[1,128,2,2048]{3,1,2,0:T(8,128)}) %all-gather.6.cloned.1.call-update) | async-done | bytes 2097168 | tf_op jit(solution)/shard_map/all_gather | solution.py:46
  238.7 3.1 select_bitcast_fusion
  242.1 86.3 %all-reduce.3.cloned.1.call-done = f32[128,2,2048]{2,0,1:T(8,128)} async-done(((f32[128,2,2048]{2,0,1:T(8,128)}), f32[128,2,2048]{2,0,1:T(8,128)}) %all-reduce.3.cloned.1.call-update) | async-done | bytes 2097168 | tf_op jit(solution)/shard_map/psum | solution.py:11
  328.4 33.0 %fusion.15 = f32[128,2,2,2048]{3,0,2,1:T(8,128)S(1)} fusion(f32[2,2048,2048]{2,1,0:T(8,128)} %param.14, f32[128,2,2048]{2,0,1:T(8,128)} %all-reduce.3.cloned.1.call-done), kind=kOutput, calls=%fused_computation.21 | convolution fusion | flops 25769803776 | bytes 39845888 | tf_op jit(solution)/shard_map/sck,dik->scdi/dot_general | solution.py:56
  361.7 1.5 pad_maximum_fusion
  363.2 1.0 copy-done.1
  364.6 29.1 %reduce-scatter.6.cloned.1.call-done = f32[32,2,2048]{2,0,1:T(8,128)} async-done(((f32[128,2,2048]{2,0,1:T(8,128)}), f32[32,2,2048]{2,0,1:T(8,128)}) %reduce-scatter.6.cloned.1.call-update) | async-done | bytes 524304 | tf_op jit(solution)/shard_map/reduce_scatter | solution.py:54
  393.7 1.2 multiply_subtract_fusion.1
  394.9 0.9 maximum_subtract_fusion
  395.9 22.7 %all-gather.4.cloned.1.call-done = f32[128,2,2048]{2,0,1:T(8,128)} async-done(((f32[32,2,2048]{2,0,1:T(8,128)}), f32[128,2,2048]{2,0,1:T(8,128)}) %all-gather.4.cloned.1.call-update) | async-done | bytes 2097168 | tf_op jit(solution)/shard_map/all_gather | solution.py:46
  418.6 3.1 broadcast_select_fusion
  422.0 86.3 %all-reduce.5.cloned.1.call-done = f32[128,2,2048]{2,0,1:T(8,128)} async-done(((f32[128,2,2048]{2,0,1:T(8,128)}), f32[128,2,2048]{2,0,1:T(8,128)}) %all-reduce.5.cloned.1.call-update) | async-done | bytes 2097168 | tf_op jit(solution)/shard_map/psum | solution.py:11
  508.3 33.0 %fusion.13 = f32[128,2,2,2048]{3,0,2,1:T(8,128)S(1)} fusion(f32[2,2048,2048]{2,1,0:T(8,128)} %param.14, f32[128,2,2048]{2,0,1:T(8,128)} %all-reduce.5.cloned.1.call-done), kind=kOutput, calls=%fused_computation.19 | convolution fusion | flops 25769803776 | bytes 39845888 | tf_op jit(solution)/shard_map/sck,dik->scdi/dot_general | solution.py:56
  541.5 1.5 pad_maximum_fusion.1
  543.0 30.5 %reduce-scatter.8.cloned.1.call-done = f32[32,2,2048]{2,0,1:T(8,128)} async-done(((f32[128,2,2048]{2,0,1:T(8,128)}), f32[32,2,2048]{2,0,1:T(8,128)}) %reduce-scatter.8.cloned.1.call-update) | async-done | bytes 524304 | tf_op jit(solution)/shard_map/reduce_scatter | solution.py:54
  573.6 1.2 multiply_subtract_fusion
  574.9 1.2 copy.21
  (51 shorter events, 2.8 us)
Async XLA Ops:
  6.5 208.6 %reduce-scatter.4.cloned.1.call-start = ((), (), s32[]{:S(2)}) async-start(), calls=%async_computation.3 | async-start | bytes 2621440 | tf_op jit(solution)/shard_map/reduce_scatter | solution.py:72
  10.3 4.4 copy-start.2
  10.3 4.3 copy-start.3
  50.5 4.4 copy-start.2
  50.5 4.3 copy-start.3
  90.7 4.4 copy-start.2
  90.7 4.3 copy-start.3
  130.9 4.4 copy-start.2
  130.9 4.3 copy-start.3
  168.4 70.3 %all-gather.6.cloned.1.call-start = ((), (), s32[]{:S(2)}) async-start(), calls=%async_computation.9 | async-start | bytes 2621440 | tf_op jit(solution)/shard_map/all_gather | solution.py:46
  215.2 113.2 %all-reduce.3.cloned.1.call-start = ((), (), s32[]{:S(2)}) async-start(), calls=%async_computation.4 | async-start | bytes 4194304 | tf_op jit(solution)/shard_map/psum | solution.py:11
  241.9 151.8 %reduce-scatter.6.cloned.1.call-start = ((), (), s32[]{:S(2)}) async-start(), calls=%async_computation.5 | async-start | bytes 2621440 | tf_op jit(solution)/shard_map/reduce_scatter | solution.py:54
  363.1 1.0 copy-start.1
  363.1 31.8 %copy-start = (f32[1,32,2,2048]{3,1,2,0:T(8,128)S(1)}, f32[1,32,2,2048]{3,1,2,0:T(8,128)}, u32[]{:S(2)}) copy-start(f32[1,32,2,2048]{3,1,2,0:T(8,128)} %reduce-scatter.4.cloned.1.call-done) | copy-start | bytes 1572868
  363.2 55.4 %all-gather.4.cloned.1.call-start = ((), (), s32[]{:S(2)}) async-start(), calls=%async_computation.6 | async-start | bytes 2621440 | tf_op jit(solution)/shard_map/all_gather | solution.py:46
  395.8 112.5 %all-reduce.5.cloned.1.call-start = ((), (), s32[]{:S(2)}) async-start(), calls=%async_computation.7 | async-start | bytes 4194304 | tf_op jit(solution)/shard_map/psum | solution.py:11
  421.7 151.8 %reduce-scatter.8.cloned.1.call-start = ((), (), s32[]{:S(2)}) async-start(), calls=%async_computation.8 | async-start | bytes 2621440 | tf_op jit(solution)/shard_map/reduce_scatter | solution.py:54
Sparse Core Ops, SparseCore 0:
  168.5 46.5 reduce-scatter.3
  216.8 21.8 all-gather.5
  242.0 86.3 all-reduce.2
  363.3 30.3 reduce-scatter.5
  395.9 22.5 all-gather.3
  421.9 86.3 all-reduce.4
  543.2 30.3 reduce-scatter.7
where the time goes:
time: 584 us; the launch traced here: 583 us
  waiting for transfers between devices  325 us (56%)
  matrix products  146 us (25%)
  other arithmetic  73.9 us (13%)
  local copies, waits for them, and re-layouts  23.4 us (4%)
  between operations  13.6 us (2%)
    psum x2, waiting for transfers between devices, from_root(): return lax.psum(kept, axis)  173 us
    dot_general x4, matrix products, interpolate(): jnp.einsum('sct,tdb->scdb', values, matrix, precision=lax.Precision.HIGHEST)  79.2 us
    dot_general x2, matrix products, multiply(): jnp.einsum('sck,dik->scdi', columns, aperture, precision=lax.Precision.HI...  66 us
    reduce_scatter x2, waiting for transfers between devices, multiply(): lax.psum_scatter(complex_join(jnp.einsum('sck,dik->scdi', columns, apertu...  59.7 us
    mul x4, other arithmetic, bin_matrix(): matrix = group_hot[:, None, :, None] * weights[:, :, None, :]  48.9 us
    reduce_scatter x1, waiting for transfers between devices, per_device(): lax.psum_scatter(lax.map(one_owner, jnp.arange(1 * lax.axis_size('rcv'),...  46.7 us
    all_gather x2, waiting for transfers between devices, to_columns(): shots_all = lax.all_gather(panel_now, 'src', axis=0, tiled=True)  46.2 us
    mul x4, local copies, waits for them, and re-layouts, bin_matrix(): matrix = group_hot[:, None, :, None] * weights[:, :, None, :]  17.3 us
  transfers between devices with their start and end apart: 7, of which 7 were waited for; matrix products, arithmetic and copies ran while one was open for 0% of the time, Pallas kernels for 0%

commit v1 on v0

v1 whole, which is shorter than its diff:
```python
import functools

import jax
import jax.numpy as jnp
from jax import lax
from jax.experimental import pallas as pl
from jax.experimental.pallas import tpu as pltpu
from jax.sharding import PartitionSpec as P

ITERS = 2
NT = (((1,), (1,)), ((), ()))
NN = (((1,), (0,)), ((), ()))
LANES = 128
VMEM_LIMIT = 56 * 2**20


def split(value):
    high = value.astype(jnp.bfloat16)
    return high, (value - high.astype(jnp.float32)).astype(jnp.bfloat16)


def dot(left, right, dims):
    return lax.dot_general(left, right, dims, preferred_element_type=jnp.float32)


def swap(value, axis, flip):
    size = lax.axis_size(axis)
    return lax.ppermute(value, axis, [(i, i ^ flip) for i in range(size)])


def bits(size):
    return [1 << b for b in range(size.bit_length() - 1)]


def line_gather(value):
    size = lax.axis_size("rcv")
    me = lax.axis_index("rcv")
    got = {0: value}
    for flip in range(1, size, 2):
        got[flip] = swap(value, "rcv", flip)
    for flip in range(2, size, 2):
        near = [abs((i ^ 1) - (i ^ flip)) < abs(i - (i ^ flip)) for i in range(size)]
        direct = lax.ppermute(value, "rcv", [(i ^ flip, i) for i in range(size) if not near[i]])
        relay = lax.ppermute(got[flip ^ 1], "rcv", [(i ^ 1, i) for i in range(size) if near[i]])
        got[flip] = jnp.where(jnp.asarray(near)[me], relay, direct)
    return [got[flip] for flip in range(size)]


def src_gather(value):
    size = lax.axis_size("src")
    got = {0: value}
    for flip in bits(size)[1:] + bits(size)[:1]:
        for key in list(got):
            got[key ^ flip] = swap(got[key], "src", flip)
    return [got[flip] for flip in range(size)]


def src_reduce(pieces):
    size = lax.axis_size("src")
    pieces = dict(enumerate(pieces))
    for flip in bits(size):
        keep = [key for key in pieces if not key & flip]
        pieces = {key: pieces[key] + swap(pieces[key ^ flip], "src", flip) for key in keep}
    return pieces[0]


def bin_kernel(n_group, n_src, first, last, *refs):
    code_ref, matrix_ref, refs = refs[0], refs[1], refs[2:]
    sum_ref, refs = (None, refs) if first else (refs[0], refs[1:])
    piece_refs, (out_ref, high, low) = refs[: n_group * n_src], refs[n_group * n_src :]
    rows, length = piece_refs[0].shape
    step = pl.program_id(0)

    @pl.when(step == 0)
    def _():
        for m in range(n_group):
            for q in range(n_src):
                here = (pl.ds(q * rows, rows), pl.ds(m * length, length))
                high[here], low[here] = split(piece_refs[m * n_src + q][...])

    codes = matrix_ref.shape[1]
    wanted = lax.broadcasted_iota(jnp.int32, (codes, 1), 0) + step * codes
    total = None if first else sum_ref[...]
    for m in range(n_group):
        part = slice(m * length, (m + 1) * length)
        hot = jnp.where(code_ref[m : m + 1, :] == wanted, 1.0, 0.0).astype(jnp.bfloat16)
        term = dot(high[:, part], hot, NT) + dot(low[:, part], hot, NT)
        total = term if total is None else total + term
    if not last:
        out_ref[...] = total
        return
    sum_high, sum_low = split(total)
    both = []
    for d in range(2):
        mat_high, mat_low = split(matrix_ref[d])
        both.append(
            dot(sum_high, mat_high, NN) + dot(sum_high, mat_low, NN) + dot(sum_low, mat_high, NN)
        )
    half = rows // 2
    for q in range(n_src):
        re, im = slice(q * rows, q * rows + half), slice(q * rows + half, (q + 1) * rows)
        out_ref[re, :] = both[0][re] - both[1][im]
        out_ref[im, :] = both[1][re] + both[0][im]


def bin_columns(blocks, codes, moveout, groups):
    n_rcv, n_src = len(blocks), lax.axis_size("src")
    rows, length = blocks[0].shape
    _, tables, stencil = moveout.shape
    per_tile = LANES // stencil
    matrix = jnp.einsum("ab,dkj->dakbj", jnp.eye(per_tile, dtype=jnp.float32), moveout,
                        precision=lax.Precision.HIGHEST)
    matrix = matrix.reshape(2, per_tile * tables, LANES)
    whole = lambda shape: pl.BlockSpec(shape, lambda i: (0,) * len(shape))
    tiled = lambda width: pl.BlockSpec((n_src * rows, width), lambda i: (0, i))
    n_group = min(2, n_rcv)
    sums, done = [], []
    for start in range(0, n_rcv, n_group):
        first, last = start == 0, start + n_group == n_rcv
        group = blocks[start : start + n_group]
        if len(done) >= 2:
            group = lax.optimization_barrier((group, done[-2]))[0]
        flat = [piece for block in group for piece in src_gather(block)]
        here = codes[start : start + n_group]
        width = LANES if last else per_tile * tables
        kernel = functools.partial(bin_kernel, n_group, n_src, first, last)
        total = pl.pallas_call(
            kernel,
            grid=(groups // per_tile,),
            in_specs=[whole(here.shape), whole(matrix.shape)]
            + [tiled(per_tile * tables) for _ in sums]
            + [whole(p.shape) for p in flat],
            out_specs=tiled(width),
            out_shape=jax.ShapeDtypeStruct((n_src * rows, groups // per_tile * width), jnp.float32),
            scratch_shapes=[pltpu.VMEM((n_src * rows, n_group * length), jnp.bfloat16)] * 2,
            compiler_params=pltpu.CompilerParams(vmem_limit_bytes=VMEM_LIMIT),
            name="bin_traces",
        )(here, matrix, *sums, *flat)
        sums = [total]
        done.append(total)
    return sums[0]


def multiply_kernel(n_src, a_ref, x_ref, out_ref, high, low):
    rows = x_ref.shape[0] // n_src
    half = rows // 2

    @pl.when(pl.program_id(0) == 0)
    def _():
        for q in range(n_src):
            re, im = pl.ds(q * rows, half), pl.ds(q * rows + half, half)
            real, imag = x_ref[re, :], x_ref[im, :]
            for d, top, bottom in ((0, real, imag), (1, -imag, real)):
                high[d, re, :], low[d, re, :] = split(top)
                high[d, im, :], low[d, im, :] = split(bottom)

    total = None
    for d in range(2):
        a_high, a_low = split(a_ref[d])
        term = dot(high[d], a_high, NT) + dot(low[d], a_high, NT) + dot(high[d], a_low, NT)
        total = term if total is None else total + term
    out_ref[...] = total


def multiply(columns, aperture):
    n_src = lax.axis_size("src")
    _, out_bins, depth = aperture.shape
    tile = min(512, out_bins)
    return pl.pallas_call(
        lambda *refs: multiply_kernel(n_src, *refs),
        grid=(out_bins // tile,),
        in_specs=[
            pl.BlockSpec((2, tile, depth), lambda i: (0, i, 0)),
            pl.BlockSpec(columns.shape, lambda i: (0, 0)),
        ],
        out_specs=pl.BlockSpec((columns.shape[0], tile), lambda i: (0, i)),
        out_shape=jax.ShapeDtypeStruct((columns.shape[0], out_bins), jnp.float32),
        scratch_shapes=[pltpu.VMEM((2,) + columns.shape, jnp.bfloat16)] * 2,
        compiler_params=pltpu.CompilerParams(vmem_limit_bytes=VMEM_LIMIT),
        name="multiply",
    )(aperture, columns)


def complex_product(left, right):
    return jnp.stack([left[0] * right[0] - left[1] * right[1], left[0] * right[1] + left[1] * right[0]])


def per_device(traces, moveout, trace_owner, trace_group, trace_table, aperture, shaping):
    n_rcv, n_src = lax.axis_size("rcv"), lax.axis_size("src")
    rcv, src = lax.axis_index("rcv"), lax.axis_index("src")
    fold = n_rcv // n_src
    shots, _, length = traces.shape
    _, tables, stencil = moveout.shape
    out_bins = aperture.shape[1]
    groups = out_bins // stencil
    rows = 2 * shots

    values = traces.transpose(1, 0, 2).reshape(rows, length)
    code = ((trace_owner * groups + trace_group) * tables + trace_table).reshape(1, length)
    codes = jnp.concatenate(line_gather(code), axis=0) - src * (fold * groups * tables)
    columns = bin_columns(line_gather(values), codes, moveout, fold * groups)

    pairs = [
        (r * n_src + s, (fold * s + r // n_src) * n_src + r % n_src)
        for r in range(n_rcv)
        for s in range(n_src)
    ]
    own = lax.dynamic_slice(
        columns, (((rcv % n_src) ^ src) * rows, (rcv // n_src) * out_bins), (rows, out_bins)
    )
    binned = lax.ppermute(own, ("rcv", "src"), pairs).reshape(2, shots, out_bins)
    shape_now = shaping.transpose(1, 0, 2)

    for sweep in range(ITERS):
        partial = multiply(columns, aperture)
        mine = src_reduce([partial[q * rows : (q + 1) * rows] for q in range(n_src)])
        panel = binned - complex_product(shape_now, mine.reshape(2, shots, out_bins))
        if sweep == ITERS - 1:
            return panel.transpose(1, 0, 2)
        blocks = jnp.stack(line_gather(panel.reshape(rows, out_bins)))
        parts = []
        for flip in range(n_src):
            for offset in range(fold):
                index = (fold * (src ^ flip) + offset) ^ rcv
                block = lax.dynamic_index_in_dim(blocks, index, 0, keepdims=False)
                parts.append(block if flip == 0 else swap(block, "src", flip))
        columns = jnp.concatenate(
            [jnp.concatenate(parts[q * fold : (q + 1) * fold], axis=1) for q in range(n_src)], axis=0
        )


def solution(mesh):
    in_specs = (
        P(("freq", "src"), None, "rcv"),
        P(None, "freq", None),
        P(("freq", "rcv")),
        P(("freq", "rcv")),
        P(("freq", "rcv")),
        P(None, ("freq", "rcv"), "src"),
        P(("freq", "src"), None, "rcv"),
    )
    out_specs = P(("freq", "src"), None, "rcv")
    return jax.shard_map(
        per_device, mesh=mesh, in_specs=in_specs, out_specs=out_specs, check_vma=False
    )
```

time: 584 us -> 284 us (0.49)
  waiting for transfers between devices: 325 us -> 97.4 us
  matrix products: 146 us -> 0 us
  starting transfers between devices: 0.65 us -> 84.8 us
  Pallas kernels: 0 us -> 79.6 us
  other arithmetic: 73.9 us -> 8.97 us
  between operations: 13.6 us -> 0.46 us
  local copies, waits for them, and re-layouts: 23.4 us -> 12.2 us
    psum x2 -> x0, waiting for transfers between devices: 173 us -> none  [from_root(): return lax.psum(kept, axis)]
    dot_general x6 -> x0, matrix products: 145 us -> none  [the longest x4 79.2 us: interpolate(): jnp.einsum('sct,tdb->scdb', values, matrix, precision=lax.Precision.HIGHEST)]
    reduce_scatter x3 -> x0, waiting for transfers between devices: 106 us -> none  [the longest x2 59.7 us: multiply(): lax.psum_scatter(complex_join(jnp.einsum('sck,dik->scdi', columns, apertu...]
    ppermute x0 -> x34, waiting for transfers between devices: none -> 97.4 us  [the longest x27 83 us: swap(): return lax.ppermute(value, axis, [(i, i ^ flip) for i in range(size)])]
    ppermute x0 -> x34, starting transfers between devices: none -> 84.8 us  [the longest x27 54.7 us: swap(): return lax.ppermute(value, axis, [(i, i ^ flip) for i in range(size)])]
    pallas_call x0 -> x4, Pallas kernels: none -> 79.6 us  [the longest x2 40.9 us: bin_columns(): pl.pallas_call(kernel, grid=(groups // per_tile,), in_specs=[whole(here.s...]
    mul x8 -> x0, other arithmetic: 51.8 us -> none  [the longest x4 48.9 us: bin_matrix(): matrix = group_hot[:, None, :, None] * weights[:, :, None, :]]
    all_gather x2 -> x0, waiting for transfers between devices: 46.2 us -> none  [to_columns(): shots_all = lax.all_gather(panel_now, 'src', axis=0, tiled=True)]
  transfers between devices with their start and end apart: 7 -> 34, of which waited for: 7 -> 14; matrix products, arithmetic and copies ran while one was open for 0% -> 4% of each run, Pallas kernels for 0% -> 5%
where the time goes in v1:
time: 284 us; the launch traced here: 283 us
  waiting for transfers between devices  97.4 us (34%)
  starting transfers between devices  84.8 us (30%)
  Pallas kernels  79.6 us (28%)
  local copies, waits for them, and re-layouts  12.2 us (4%)
  other arithmetic  8.97 us (3%)
    ppermute x27, waiting for transfers between devices, swap(): return lax.ppermute(value, axis, [(i, i ^ flip) for i in range(size)])  83 us
    ppermute x27, starting transfers between devices, swap(): return lax.ppermute(value, axis, [(i, i ^ flip) for i in range(size)])  54.7 us
    pallas_call x2, Pallas kernels, bin_columns(): pl.pallas_call(kernel, grid=(groups // per_tile,), in_specs=[whole(here.s...  40.9 us
    pallas_call x2, Pallas kernels, multiply(): pl.pallas_call(lambda *refs: multiply_kernel(n_src, *refs), grid=(out_bin...  38.7 us
    ppermute x3, starting transfers between devices, line_gather(): lax.ppermute(value, 'rcv', [(i ^ flip, i) for i in range(size) if not nea...  25.4 us
    ppermute x3, waiting for transfers between devices, line_gather(): lax.ppermute(got[flip ^ 1], 'rcv', [(i ^ 1, i) for i in range(size) if ne...  14.4 us
  transfers between devices with their start and end apart: 34, of which 14 were waited for; matrix products, arithmetic and copies ran while one was open for 4% of the time, Pallas kernels for 5%

profile of v1, /device:TPU:0, one launch (start us, length us, event | category | flops | bytes accessed | tf_op | source)
XLA Modules:
  0.0 283.4 jit_solution(5720298668150402234)
XLA Ops:
  0.0 1.0 copy.15
  1.0 5.1 %collective-permute-start.11 = (f32[64,1024]{1,0:T(8,128)S(1)}, f32[64,1024]{1,0:T(8,128)S(1)}, u32[]{:S(2)}, u32[]{:S(2)}) collective-permute-start(f32[64,1024]{1,0:T(8,128)S(1)} %bitcast.63), channel_id=1, source_target_pairs={{0,12},{4,8},{8,4},{12,0},{1,13},{5,9},{9,5},{13,1},{2,14},{6,10},... | collective-permute-start | bytes 786440 | tf_op jit(solution)/shard_map/ppermute | solution.py:28
  6.2 1.3 collective-permute-start.13
  7.5 5.9 %collective-permute-done.11.refs_7_ = f32[64,1024]{1,0:T(8,128)S(1)} collective-permute-done((f32[64,1024]{1,0:T(8,128)S(1)}, f32[64,1024]{1,0:T(8,128)S(1)}, u32[]{:S(2)}, u32[]{:S(2)}) %collective-permute-start.11) | collective-permute-done | bytes 262176 | tf_op jit(solution)/shard_map/ppermute | solution.py:28
  13.4 1.3 collective-permute-start.12
  14.7 0.7 multiply_add_fusion
  15.4 3.8 %collective-permute-start.1 = (s32[1,1024]{1,0:T(1,128)S(1)}, s32[1,1024]{1,0:T(1,128)S(1)}, u32[]{:S(2)}, u32[]{:S(2)}) collective-permute-start(s32[1,1024]{1,0:T(1,128)S(1)} %bitcast.71), channel_id=1, source_target_pairs={{0,12},{4,8},{8,4},{12,0},{1,13},{5,9},{9,5},{13,1},{2,14},{6,10},... | collective-permute-start | bytes 12296 | tf_op jit(solution)/shard_map/ppermute | solution.py:28
  19.2 9.7 %collective-permute-start.3 = (s32[1,1024]{1,0:T(1,128)S(1)}, s32[1,1024]{1,0:T(1,128)S(1)}, u32[]{:S(2)}, u32[]{:S(2)}) collective-permute-start(s32[1,1024]{1,0:T(1,128)S(1)} %bitcast.72), channel_id=1, source_target_pairs={{12,4},{0,8},{13,5},{1,9},{14,6},{2,10},{15,7},{3,11},{28,20},{16,... | collective-permute-start | bytes 12296 | tf_op jit(solution)/shard_map/ppermute | solution.py:43
  29.0 1.6 collective-permute-start.5
  30.6 1.3 dynamic_slice.26
  31.8 3.0 %collective-permute-start = (s32[1,1024]{1,0:T(1,128)S(1)}, s32[1,1024]{1,0:T(1,128)S(1)}, u32[]{:S(2)}, u32[]{:S(2)}) collective-permute-start(s32[1,1024]{1,0:T(1,128)S(1)} %bitcast.73), channel_id=1, source_target_pairs={{0,4},{4,0},{8,12},{12,8},{1,5},{5,1},{9,13},{13,9},{2,6},{6,2},{1... | collective-permute-start | bytes 12296 | tf_op jit(solution)/shard_map/ppermute | solution.py:28
  34.9 1.3 collective-permute-start.2
  36.8 1.6 collective-permute-start.9
  38.4 2.0 collective-permute-done.2
  40.4 1.5 collective-permute-start.18
  42.5 0.9 multiply_bitcast_fusion
  43.7 0.8 copy.17.refs_1_
  45.2 0.9 collective-permute-done.9.refs_8_
  46.6 5.0 %collective-permute-done.18.refs_9_ = f32[64,1024]{1,0:T(8,128)S(1)} collective-permute-done((f32[64,1024]{1,0:T(8,128)S(1)}, f32[64,1024]{1,0:T(8,128)S(1)}, u32[]{:S(2)}, u32[]{:S(2)}) %collective-permute-start.18) | collective-permute-done | bytes 262176 | tf_op jit(solution)/shard_map/ppermute | solution.py:28
  51.7 5.0 %collective-permute-done.15.refs_5_ = f32[64,1024]{1,0:T(8,128)} collective-permute-done((f32[64,1024]{1,0:T(8,128)S(1)}, f32[64,1024]{1,0:T(8,128)}, u32[]{:S(2)}, u32[]{:S(2)}) %collective-permute-start.15) | collective-permute-done | bytes 262176 | tf_op jit(solution)/shard_map/ppermute | solution.py:28
  58.0 15.3 %bin_traces.2.refs_2_ = f32[256,4096]{1,0:T(8,128)} custom-call(s32[2,1024]{1,0:T(2,128)} %get-tuple-element.17.refs_0_, f32[2,256,128]{2,1,0:T(8,128)} %copy.17.refs_1_, f32[64,1024]{1,0:T(8,128)} %bitcast.68, f32[64,1024]{1,0:T(8,128)} %copy-done.8, f32[64,1024]{1,0:T(8,128)} %copy-done.7, f32[64,1024]{1,0:T(8,128)} %collective-permute-done.6.refs_5_, ...), custom_call_target="tpu_custom_call" | custom-call | tf_op jit(solution)/shard_map/bin_traces/pallas_call | solution.py:127
  74.4 25.7 %bin_traces.3.refs_1_ = f32[256,2048]{1,0:T(8,128)} custom-call(s32[2,1024]{1,0:T(2,128)} %get-tuple-element.18.refs_0_, f32[2,256,128]{2,1,0:T(8,128)} %copy.17.refs_1_, f32[256,4096]{1,0:T(8,128)} %bin_traces.2.refs_2_, f32[64,1024]{1,0:T(8,128)} %copy-done.3, f32[64,1024]{1,0:T(8,128)} %copy-done.12, f32[64,1024]{1,0:T(8,128)} %collective-permute-done.15.refs_5_, ...), custom_call_target="tpu_custom_call" | custom-call | tf_op jit(solution)/shard_map/bin_traces/pallas_call | solution.py:127
  100.0 19.4 %multiply.3 = f32[256,2048]{1,0:T(8,128)} custom-call(f32[2,2048,2048]{2,1,0:T(8,128)} %refs_0_.3, f32[256,2048]{1,0:T(8,128)} %bin_traces.3.refs_1_), custom_call_target="tpu_custom_call" | custom-call | tf_op jit(solution)/shard_map/multiply/pallas_call | solution.py:169
  119.4 2.2 fusion.5
  122.2 2.2 collective-permute-done.22
  124.3 0.9 slice_add_fusion.2
  125.2 1.5 collective-permute-start.23
  127.1 1.1 constant_dynamic-slice_fusion
  128.1 0.7 collective-permute-start.20
  128.9 15.5 %collective-permute-done.23 = f32[64,2048]{1,0:T(8,128)} collective-permute-done((f32[64,2048]{1,0:T(8,128)}, f32[64,2048]{1,0:T(8,128)}, u32[]{:S(2)}, u32[]{:S(2)}) %collective-permute-start.23) | collective-permute-done | bytes 524320 | tf_op jit(solution)/shard_map/ppermute | solution.py:28
  144.4 1.3 fusion.1
  145.9 3.6 %collective-permute-start.25 = (f32[64,2048]{1,0:T(8,128)S(1)}, f32[64,2048]{1,0:T(8,128)S(1)}, u32[]{:S(2)}, u32[]{:S(2)}) collective-permute-start(f32[64,2048]{1,0:T(8,128)S(1)} %bitcast_subtract_fusion), channel_id=1, source_target_pairs={{0,12},{4,8},{8,4},{12,0},{1,13},{5,9},{9,5},{13,1},{2,14},{6,10},... | collective-permute-start | bytes 1572872 | tf_op jit(solution)/shard_map/ppermute | solution.py:28
  149.5 14.4 %collective-permute-start.27 = (f32[64,2048]{1,0:T(8,128)S(1)}, f32[64,2048]{1,0:T(8,128)S(1)}, u32[]{:S(2)}, u32[]{:S(2)}) collective-permute-start(f32[64,2048]{1,0:T(8,128)S(1)} %bitcast_subtract_fusion), channel_id=1, source_target_pairs={{12,4},{0,8},{13,5},{1,9},{14,6},{2,10},{15,7},{3,11},{28,20},{16,... | collective-permute-start | bytes 1572872 | tf_op jit(solution)/shard_map/ppermute | solution.py:43
  163.9 1.5 collective-permute-start.26
  165.4 28.2 %collective-permute-start.24 = (f32[64,2048]{1,0:T(8,128)S(1)}, f32[64,2048]{1,0:T(8,128)}, u32[]{:S(2)}, u32[]{:S(2)}) collective-permute-start(f32[64,2048]{1,0:T(8,128)S(1)} %bitcast_subtract_fusion), channel_id=1, source_target_pairs={{0,4},{4,0},{8,12},{12,8},{1,5},{5,1},{9,13},{13,9},{2,6},{6,2},{1... | collective-permute-start | bytes 1572872 | tf_op jit(solution)/shard_map/ppermute | solution.py:28
  193.6 12.4 %collective-permute-done.26 = f32[64,2048]{1,0:T(8,128)S(1)} collective-permute-done((f32[64,2048]{1,0:T(8,128)S(1)}, f32[64,2048]{1,0:T(8,128)S(1)}, u32[]{:S(2)}, u32[]{:S(2)}) %collective-permute-start.26) | collective-permute-done | bytes 524320 | tf_op jit(solution)/shard_map/ppermute | solution.py:44
  206.0 0.7 select_bitcast_fusion
  206.7 10.2 %collective-permute-done.24 = f32[64,2048]{1,0:T(8,128)} collective-permute-done((f32[64,2048]{1,0:T(8,128)S(1)}, f32[64,2048]{1,0:T(8,128)}, u32[]{:S(2)}, u32[]{:S(2)}) %collective-permute-start.24) | collective-permute-done | bytes 524320 | tf_op jit(solution)/shard_map/ppermute | solution.py:28
  216.8 1.2 pad_maximum_fusion
  218.4 1.8 collective-permute-start.30
  220.2 12.9 %collective-permute-done.29 = f32[64,2048]{1,0:T(8,128)S(1)} collective-permute-done((f32[64,2048]{1,0:T(8,128)S(1)}, f32[64,2048]{1,0:T(8,128)S(1)}, u32[]{:S(2)}, u32[]{:S(2)}) %collective-permute-start.29) | collective-permute-done | bytes 524320 | tf_op jit(solution)/shard_map/ppermute | solution.py:28
  233.1 10.3 %collective-permute-done.30 = f32[64,2048]{1,0:T(8,128)S(1)} collective-permute-done((f32[64,2048]{1,0:T(8,128)S(1)}, f32[64,2048]{1,0:T(8,128)S(1)}, u32[]{:S(2)}, u32[]{:S(2)}) %collective-permute-start.30) | collective-permute-done | bytes 524320 | tf_op jit(solution)/shard_map/ppermute | solution.py:28
  243.5 1.6 pad_maximum_fusion.1.refs_1_
  245.0 19.3 %multiply.4 = f32[256,2048]{1,0:T(8,128)} custom-call(f32[2,2048,2048]{2,1,0:T(8,128)} %refs_0_.3, f32[256,2048]{1,0:T(8,128)} %pad_maximum_fusion.1.refs_1_), custom_call_target="tpu_custom_call" | custom-call | tf_op jit(solution)/shard_map/multiply/pallas_call | solution.py:169
  264.3 1.4 fusion.4
  266.3 1.4 collective-permute-done.32
  268.5 13.5 %collective-permute-done.33 = f32[64,2048]{1,0:T(8,128)S(1)} collective-permute-done((f32[64,2048]{1,0:T(8,128)S(1)}, f32[64,2048]{1,0:T(8,128)S(1)}, u32[]{:S(2)}, u32[]{:S(2)}) %collective-permute-start.33) | collective-permute-done | bytes 524320 | tf_op jit(solution)/shard_map/ppermute | solution.py:28
  282.2 1.2 copy.19
  (85 shorter events, 8.1 us)
Async XLA Ops:
  1.0 56.3 %copy-start.2 = (f32[2,32,1024]{2,1,0:T(8,128)}, f32[2,32,1024]{2,1,0:T(8,128)S(1)}, u32[]{:S(2)}) copy-start(f32[2,32,1024]{2,1,0:T(8,128)S(1)} %copy.15) | copy-start | bytes 786436
  1.0 12.3 %collective-permute-start.11 = (f32[64,1024]{1,0:T(8,128)S(1)}, f32[64,1024]{1,0:T(8,128)S(1)}, u32[]{:S(2)}, u32[]{:S(2)}) collective-permute-start(f32[64,1024]{1,0:T(8,128)S(1)} %bitcast.63), channel_id=1, source_target_pairs={{0,12},{4,8},{8,4},{12,0},{1,13},{5,9},{9,5},{13,1},{2,14},{6,10},... | collective-permute-start | bytes 786440 | tf_op jit(solution)/shard_map/ppermute | solution.py:28
  6.2 25.7 %collective-permute-start.13 = (f32[64,1024]{1,0:T(8,128)S(1)}, f32[64,1024]{1,0:T(8,128)S(1)}, u32[]{:S(2)}, u32[]{:S(2)}) collective-permute-start(f32[64,1024]{1,0:T(8,128)S(1)} %bitcast.64), channel_id=1, source_target_pairs={{12,4},{0,8},{13,5},{1,9},{14,6},{2,10},{15,7},{3,11},{28,20},{16,... | collective-permute-start | bytes 786440 | tf_op jit(solution)/shard_map/ppermute | solution.py:43
  13.4 59.9 %copy-start.5 = (f32[64,1024]{1,0:T(8,128)}, f32[64,1024]{1,0:T(8,128)S(1)}, u32[]{:S(2)}) copy-start(f32[64,1024]{1,0:T(8,128)S(1)} %collective-permute-done.11.refs_7_) | copy-start | bytes 786436
  13.4 21.5 %collective-permute-start.12 = (f32[64,1024]{1,0:T(8,128)S(1)}, f32[64,1024]{1,0:T(8,128)S(1)}, u32[]{:S(2)}, u32[]{:S(2)}) collective-permute-start(f32[64,1024]{1,0:T(8,128)S(1)} %collective-permute-done.11.refs_7_), channel_id=1, source_target_pairs={{4,0},{8,12},{5,1},{9,13},{6,2},{10,14},{7,3},{11,15},{20,16},{24,... | collective-permute-start | bytes 786440 | tf_op jit(solution)/shard_map/ppermute | solution.py:44
  15.4 13.6 %collective-permute-start.1 = (s32[1,1024]{1,0:T(1,128)S(1)}, s32[1,1024]{1,0:T(1,128)S(1)}, u32[]{:S(2)}, u32[]{:S(2)}) collective-permute-start(s32[1,1024]{1,0:T(1,128)S(1)} %bitcast.71), channel_id=1, source_target_pairs={{0,12},{4,8},{8,4},{12,0},{1,13},{5,9},{9,5},{13,1},{2,14},{6,10},... | collective-permute-start | bytes 12296 | tf_op jit(solution)/shard_map/ppermute | solution.py:28
  19.2 11.3 %collective-permute-start.3 = (s32[1,1024]{1,0:T(1,128)S(1)}, s32[1,1024]{1,0:T(1,128)S(1)}, u32[]{:S(2)}, u32[]{:S(2)}) collective-permute-start(s32[1,1024]{1,0:T(1,128)S(1)} %bitcast.72), channel_id=1, source_target_pairs={{12,4},{0,8},{13,5},{1,9},{14,6},{2,10},{15,7},{3,11},{28,20},{16,... | collective-permute-start | bytes 12296 | tf_op jit(solution)/shard_map/ppermute | solution.py:43
  28.9 7.9 %collective-permute-start.7 = (f32[64,1024]{1,0:T(8,128)S(1)}, f32[64,1024]{1,0:T(8,128)S(1)}, u32[]{:S(2)}, u32[]{:S(2)}) collective-permute-start(f32[64,1024]{1,0:T(8,128)S(1)} %bitcast.65), channel_id=1, source_target_pairs={{0,4},{4,0},{8,12},{12,8},{1,5},{5,1},{9,13},{13,9},{2,6},{6,2},{1... | collective-permute-start | bytes 786440 | tf_op jit(solution)/shard_map/ppermute | solution.py:28
  29.0 12.9 %collective-permute-start.5 = (f32[64,1024]{1,0:T(8,128)S(1)}, f32[64,1024]{1,0:T(8,128)S(1)}, u32[]{:S(2)}, u32[]{:S(2)}) collective-permute-start(f32[64,1024]{1,0:T(8,128)S(1)} %bitcast.66), channel_id=1, source_target_pairs={{0,2},{1,3},{2,0},{3,1},{4,6},{5,7},{6,4},{7,5},{8,10},{9,11},{10,... | collective-permute-start | bytes 786440 | tf_op jit(solution)/shard_map/ppermute | solution.py:28
  30.6 11.3 %collective-permute-start.4 = (f32[64,1024]{1,0:T(8,128)S(1)}, f32[64,1024]{1,0:T(8,128)S(1)}, u32[]{:S(2)}, u32[]{:S(2)}) collective-permute-start(f32[64,1024]{1,0:T(8,128)S(1)} %bitcast.67), channel_id=1, source_target_pairs={{0,1},{1,0},{2,3},{3,2},{4,5},{5,4},{6,7},{7,6},{8,9},{9,8},{10,11... | collective-permute-start | bytes 786440 | tf_op jit(solution)/shard_map/ppermute | solution.py:28
  31.8 6.6 %collective-permute-start = (s32[1,1024]{1,0:T(1,128)S(1)}, s32[1,1024]{1,0:T(1,128)S(1)}, u32[]{:S(2)}, u32[]{:S(2)}) collective-permute-start(s32[1,1024]{1,0:T(1,128)S(1)} %bitcast.73), channel_id=1, source_target_pairs={{0,4},{4,0},{8,12},{12,8},{1,5},{5,1},{9,13},{13,9},{2,6},{6,2},{1... | collective-permute-start | bytes 12296 | tf_op jit(solution)/shard_map/ppermute | solution.py:28
  34.9 5.5 %collective-permute-start.2 = (s32[1,1024]{1,0:T(1,128)S(1)}, s32[1,1024]{1,0:T(1,128)S(1)}, u32[]{:S(2)}, u32[]{:S(2)}) collective-permute-start(s32[1,1024]{1,0:T(1,128)S(1)} %collective-permute-done.1), channel_id=1, source_target_pairs={{4,0},{8,12},{5,1},{9,13},{6,2},{10,14},{7,3},{11,15},{20,16},{24,... | collective-permute-start | bytes 12296 | tf_op jit(solution)/shard_map/ppermute | solution.py:44
  36.8 36.5 %copy-start.3 = (f32[64,1024]{1,0:T(8,128)}, f32[64,1024]{1,0:T(8,128)S(1)}, u32[]{:S(2)}) copy-start(f32[64,1024]{1,0:T(8,128)S(1)} %broadcast_select_fusion.refs_3_) | copy-start | bytes 786436
  36.8 20.5 %copy-start.6 = (f32[64,1024]{1,0:T(8,128)}, f32[64,1024]{1,0:T(8,128)S(1)}, u32[]{:S(2)}) copy-start(f32[64,1024]{1,0:T(8,128)S(1)} %collective-permute-done.7.refs_6_) | copy-start | bytes 786436
  36.8 9.2 %collective-permute-start.9 = (f32[64,1024]{1,0:T(8,128)S(1)}, f32[64,1024]{1,0:T(8,128)S(1)}, u32[]{:S(2)}, u32[]{:S(2)}) collective-permute-start(f32[64,1024]{1,0:T(8,128)S(1)} %collective-permute-done.7.refs_6_), channel_id=1, source_target_pairs={{0,2},{1,3},{2,0},{3,1},{4,6},{5,7},{6,4},{7,5},{8,10},{9,11},{10,... | collective-permute-start | bytes 786440 | tf_op jit(solution)/shard_map/ppermute | solution.py:28
  38.4 7.7 %collective-permute-start.8 = (f32[64,1024]{1,0:T(8,128)S(1)}, f32[64,1024]{1,0:T(8,128)}, u32[]{:S(2)}, u32[]{:S(2)}) collective-permute-start(f32[64,1024]{1,0:T(8,128)S(1)} %collective-permute-done.7.refs_6_), channel_id=1, source_target_pairs={{0,1},{1,0},{2,3},{3,2},{4,5},{5,4},{6,7},{7,6},{8,9},{9,8},{10,11... | collective-permute-start | bytes 786440 | tf_op jit(solution)/shard_map/ppermute | solution.py:28
  40.4 11.3 %collective-permute-start.18 = (f32[64,1024]{1,0:T(8,128)S(1)}, f32[64,1024]{1,0:T(8,128)S(1)}, u32[]{:S(2)}, u32[]{:S(2)}) collective-permute-start(f32[64,1024]{1,0:T(8,128)S(1)} %collective-permute-done.11.refs_7_), channel_id=1, source_target_pairs={{0,2},{1,3},{2,0},{3,1},{4,6},{5,7},{6,4},{7,5},{8,10},{9,11},{10,... | collective-permute-start | bytes 786440 | tf_op jit(solution)/shard_map/ppermute | solution.py:28
  41.9 15.5 %copy-start.7 = (f32[64,1024]{1,0:T(8,128)}, f32[64,1024]{1,0:T(8,128)S(1)}, u32[]{:S(2)}) copy-start(f32[64,1024]{1,0:T(8,128)S(1)} %collective-permute-done.5.refs_4_) | copy-start | bytes 786436
  41.9 4.7 %collective-permute-start.6 = (f32[64,1024]{1,0:T(8,128)S(1)}, f32[64,1024]{1,0:T(8,128)}, u32[]{:S(2)}, u32[]{:S(2)}) collective-permute-start(f32[64,1024]{1,0:T(8,128)S(1)} %collective-permute-done.5.refs_4_), channel_id=1, source_target_pairs={{0,1},{1,0},{2,3},{3,2},{4,5},{5,4},{6,7},{7,6},{8,9},{9,8},{10,11... | collective-permute-start | bytes 786440 | tf_op jit(solution)/shard_map/ppermute | solution.py:28
  41.9 15.5 %copy-start.8 = (f32[64,1024]{1,0:T(8,128)}, f32[64,1024]{1,0:T(8,128)S(1)}, u32[]{:S(2)}) copy-start(f32[64,1024]{1,0:T(8,128)S(1)} %collective-permute-done.4.refs_3_) | copy-start | bytes 786436
  41.9 14.8 %collective-permute-start.15 = (f32[64,1024]{1,0:T(8,128)S(1)}, f32[64,1024]{1,0:T(8,128)}, u32[]{:S(2)}, u32[]{:S(2)}) collective-permute-start(f32[64,1024]{1,0:T(8,128)S(1)} %broadcast_select_fusion.refs_3_), channel_id=1, source_target_pairs={{0,2},{1,3},{2,0},{3,1},{4,6},{5,7},{6,4},{7,5},{8,10},{9,11},{10,... | collective-permute-start | bytes 786440 | tf_op jit(solution)/shard_map/ppermute | solution.py:28
  46.1 11.3 %copy-start.10 = (f32[64,1024]{1,0:T(8,128)}, f32[64,1024]{1,0:T(8,128)S(1)}, u32[]{:S(2)}) copy-start(f32[64,1024]{1,0:T(8,128)S(1)} %collective-permute-done.9.refs_8_) | copy-start | bytes 786436
  46.1 27.3 %collective-permute-start.17 = (f32[64,1024]{1,0:T(8,128)S(1)}, f32[64,1024]{1,0:T(8,128)S(1)}, u32[]{:S(2)}, u32[]{:S(2)}) collective-permute-start(f32[64,1024]{1,0:T(8,128)S(1)} %collective-permute-done.11.refs_7_), channel_id=1, source_target_pairs={{0,1},{1,0},{2,3},{3,2},{4,5},{5,4},{6,7},{7,6},{8,9},{9,8},{10,11... | collective-permute-start | bytes 786440 | tf_op jit(solution)/shard_map/ppermute | solution.py:28
  46.1 27.3 %collective-permute-start.14 = (f32[64,1024]{1,0:T(8,128)S(1)}, f32[64,1024]{1,0:T(8,128)S(1)}, u32[]{:S(2)}, u32[]{:S(2)}) collective-permute-start(f32[64,1024]{1,0:T(8,128)S(1)} %broadcast_select_fusion.refs_3_), channel_id=1, source_target_pairs={{0,1},{1,0},{2,3},{3,2},{4,5},{5,4},{6,7},{7,6},{8,9},{9,8},{10,11... | collective-permute-start | bytes 786440 | tf_op jit(solution)/shard_map/ppermute | solution.py:28
  46.6 10.8 %collective-permute-start.10 = (f32[64,1024]{1,0:T(8,128)S(1)}, f32[64,1024]{1,0:T(8,128)S(1)}, u32[]{:S(2)}, u32[]{:S(2)}) collective-permute-start(f32[64,1024]{1,0:T(8,128)S(1)} %collective-permute-done.9.refs_8_), channel_id=1, source_target_pairs={{0,1},{1,0},{2,3},{3,2},{4,5},{5,4},{6,7},{7,6},{8,9},{9,8},{10,11... | collective-permute-start | bytes 786440 | tf_op jit(solution)/shard_map/ppermute | solution.py:28
  51.7 21.6 %copy-start.9 = (f32[64,1024]{1,0:T(8,128)}, f32[64,1024]{1,0:T(8,128)S(1)}, u32[]{:S(2)}) copy-start(f32[64,1024]{1,0:T(8,128)S(1)} %collective-permute-done.18.refs_9_) | copy-start | bytes 786436
  51.7 21.7 %collective-permute-start.19 = (f32[64,1024]{1,0:T(8,128)S(1)}, f32[64,1024]{1,0:T(8,128)S(1)}, u32[]{:S(2)}, u32[]{:S(2)}) collective-permute-start(f32[64,1024]{1,0:T(8,128)S(1)} %collective-permute-done.18.refs_9_), channel_id=1, source_target_pairs={{0,1},{1,0},{2,3},{3,2},{4,5},{5,4},{6,7},{7,6},{8,9},{9,8},{10,11... | collective-permute-start | bytes 786440 | tf_op jit(solution)/shard_map/ppermute | solution.py:28
  56.7 16.7 %collective-permute-start.16 = (f32[64,1024]{1,0:T(8,128)}, f32[64,1024]{1,0:T(8,128)S(1)}, u32[]{:S(2)}, u32[]{:S(2)}) collective-permute-start(f32[64,1024]{1,0:T(8,128)} %collective-permute-done.15.refs_5_), channel_id=1, source_target_pairs={{0,1},{1,0},{2,3},{3,2},{4,5},{5,4},{6,7},{7,6},{8,9},{9,8},{10,11... | collective-permute-start | bytes 786440 | tf_op jit(solution)/shard_map/ppermute | solution.py:28
  73.3 0.8 copy-start.12
  73.4 0.9 copy-start.13
  73.4 1.0 copy-start.14
  119.4 4.9 %copy-start = (f32[256,2048]{1,0:T(8,128)S(1)}, f32[256,2048]{1,0:T(8,128)}, u32[]{:S(2)}) copy-start(f32[256,2048]{1,0:T(8,128)} %multiply.3) | copy-start | bytes 6291460
  119.4 7.3 %copy-start.4 = (f32[32,2,2048]{2,1,0:T(2,128)S(1)}, f32[32,2,2048]{2,1,0:T(2,128)}, u32[]{:S(2)}) copy-start(f32[32,2,2048]{2,1,0:T(2,128)} %param.16) | copy-start | bytes 1572868
  121.6 2.7 collective-permute-start.22
  122.1 6.7 %collective-permute-start.21 = (f32[64,2048]{1,0:T(8,128)}, f32[64,2048]{1,0:T(8,128)}, u32[]{:S(2)}, u32[]{:S(2)}) collective-permute-start(f32[64,2048]{1,0:T(8,128)} %get-tuple-element.11), channel_id=1, source_target_pairs={{0,1},{1,0},{2,3},{3,2},{4,5},{5,4},{6,7},{7,6},{8,9},{9,8},{10,11... | collective-permute-start | bytes 1572872 | tf_op jit(solution)/shard_map/ppermute | solution.py:28
  125.2 19.2 %collective-permute-start.23 = (f32[64,2048]{1,0:T(8,128)}, f32[64,2048]{1,0:T(8,128)}, u32[]{:S(2)}, u32[]{:S(2)}) collective-permute-start(f32[64,2048]{1,0:T(8,128)} %slice_add_fusion.2), channel_id=1, source_target_pairs={{0,2},{1,3},{2,0},{3,1},{4,6},{5,7},{6,4},{7,5},{8,10},{9,11},{10,... | collective-permute-start | bytes 1572872 | tf_op jit(solution)/shard_map/ppermute | solution.py:28
  128.1 17.7 %collective-permute-start.20 = (f32[64,2048]{1,0:T(8,128)S(1)}, f32[64,2048]{1,0:T(8,128)S(1)}, u32[]{:S(2)}, u32[]{:S(2)}) collective-permute-start(f32[64,2048]{1,0:T(8,128)S(1)} %constant_dynamic-slice_fusion), channel_id=1, source_target_pairs={{0,0},{1,4},{2,8},{3,12},{4,1},{5,5},{6,9},{7,13},{8,2},{9,6},{10,... | collective-permute-start | bytes 1572872 | tf_op jit(solution)/shard_map/ppermute | solution.py:211
  145.9 18.0 %collective-permute-start.25 = (f32[64,2048]{1,0:T(8,128)S(1)}, f32[64,2048]{1,0:T(8,128)S(1)}, u32[]{:S(2)}, u32[]{:S(2)}) collective-permute-start(f32[64,2048]{1,0:T(8,128)S(1)} %bitcast_subtract_fusion), channel_id=1, source_target_pairs={{0,12},{4,8},{8,4},{12,0},{1,13},{5,9},{9,5},{13,1},{2,14},{6,10},... | collective-permute-start | bytes 1572872 | tf_op jit(solution)/shard_map/ppermute | solution.py:28
  149.5 44.1 %collective-permute-start.27 = (f32[64,2048]{1,0:T(8,128)S(1)}, f32[64,2048]{1,0:T(8,128)S(1)}, u32[]{:S(2)}, u32[]{:S(2)}) collective-permute-start(f32[64,2048]{1,0:T(8,128)S(1)} %bitcast_subtract_fusion), channel_id=1, source_target_pairs={{12,4},{0,8},{13,5},{1,9},{14,6},{2,10},{15,7},{3,11},{28,20},{16,... | collective-permute-start | bytes 1572872 | tf_op jit(solution)/shard_map/ppermute | solution.py:43
  163.9 42.1 %collective-permute-start.26 = (f32[64,2048]{1,0:T(8,128)S(1)}, f32[64,2048]{1,0:T(8,128)S(1)}, u32[]{:S(2)}, u32[]{:S(2)}) collective-permute-start(f32[64,2048]{1,0:T(8,128)S(1)} %collective-permute-done.25), channel_id=1, source_target_pairs={{4,0},{8,12},{5,1},{9,13},{6,2},{10,14},{7,3},{11,15},{20,16},{24,... | collective-permute-start | bytes 1572872 | tf_op jit(solution)/shard_map/ppermute | solution.py:44
  165.4 51.4 %collective-permute-start.24 = (f32[64,2048]{1,0:T(8,128)S(1)}, f32[64,2048]{1,0:T(8,128)}, u32[]{:S(2)}, u32[]{:S(2)}) collective-permute-start(f32[64,2048]{1,0:T(8,128)S(1)} %bitcast_subtract_fusion), channel_id=1, source_target_pairs={{0,4},{4,0},{8,12},{12,8},{1,5},{5,1},{9,13},{13,9},{2,6},{6,2},{1... | collective-permute-start | bytes 1572872 | tf_op jit(solution)/shard_map/ppermute | solution.py:28
  218.3 2.0 collective-permute-start.28
  218.3 14.8 %collective-permute-start.29 = (f32[64,2048]{1,0:T(8,128)S(1)}, f32[64,2048]{1,0:T(8,128)S(1)}, u32[]{:S(2)}, u32[]{:S(2)}) collective-permute-start(f32[64,2048]{1,0:T(8,128)S(1)} %get-tuple-element.9), channel_id=1, source_target_pairs={{0,2},{1,3},{2,0},{3,1},{4,6},{5,7},{6,4},{7,5},{8,10},{9,11},{10,... | collective-permute-start | bytes 1572872 | tf_op jit(solution)/shard_map/ppermute | solution.py:28
  218.4 25.0 %collective-permute-start.30 = (f32[64,2048]{1,0:T(8,128)S(1)}, f32[64,2048]{1,0:T(8,128)S(1)}, u32[]{:S(2)}, u32[]{:S(2)}) collective-permute-start(f32[64,2048]{1,0:T(8,128)S(1)} %get-tuple-element.8), channel_id=1, source_target_pairs={{0,3},{1,2},{2,1},{3,0},{4,7},{5,6},{6,5},{7,4},{8,11},{9,10},{10,... | collective-permute-start | bytes 1572872 | tf_op jit(solution)/shard_map/ppermute | solution.py:28
  264.3 3.4 %copy-start.1 = (f32[256,2048]{1,0:T(8,128)S(1)}, f32[256,2048]{1,0:T(8,128)}, u32[]{:S(2)}) copy-start(f32[256,2048]{1,0:T(8,128)} %multiply.4) | copy-start | bytes 6291460
  265.8 2.0 collective-permute-start.32
  266.1 2.4 collective-permute-start.31
  267.8 14.2 %collective-permute-start.33 = (f32[64,2048]{1,0:T(8,128)S(1)}, f32[64,2048]{1,0:T(8,128)S(1)}, u32[]{:S(2)}, u32[]{:S(2)}) collective-permute-start(f32[64,2048]{1,0:T(8,128)S(1)} %slice_add_fusion), channel_id=1, source_target_pairs={{0,2},{1,3},{2,0},{3,1},{4,6},{5,7},{6,4},{7,5},{8,10},{9,11},{10,... | collective-permute-start | bytes 1572872 | tf_op jit(solution)/shard_map/ppermute | solution.py:28
  (2 other events, 1.4 us)

commit v2 on v0

v2 whole, which is shorter than its diff:
```python
import functools

import jax
import jax.numpy as jnp
from jax import lax
from jax.experimental import pallas as pl
from jax.experimental.pallas import tpu as pltpu
from jax.sharding import PartitionSpec as P

ITERS = 2
NT = (((1,), (1,)), ((), ()))
NN = (((1,), (0,)), ((), ()))
LANES = 128
VMEM_LIMIT = 56 * 2**20


def split(value):
    high = value.astype(jnp.bfloat16)
    return high, (value - high.astype(jnp.float32)).astype(jnp.bfloat16)


def dot(left, right, dims):
    return lax.dot_general(left, right, dims, preferred_element_type=jnp.float32)


def reverse(value, size):
    out, bit = 0, size >> 1
    while bit:
        out, value, bit = out | (bit if value & 1 else 0), value >> 1, bit >> 1
    return out


def turn(value, size):
    count = size.bit_length() - 1
    return sum(((value >> b) & 1) << (count - 1 - b) for b in range(count))


def bits(size):
    return [1 << b for b in range(size.bit_length() - 1)]


def swap(value, axis, flip):
    size = lax.axis_size(axis)
    return lax.ppermute(value, axis, [(i, i ^ flip) for i in range(size)])


def line_step(by_shift, step, *others):
    size = lax.axis_size("rcv")
    up = [(i, i + 1) for i in range(step - 1, size - 1)]
    down = [(i + 1, i) for i in range(size - step)]
    below, above = after((by_shift[1 - step], by_shift[step - 1]), *others)
    by_shift[-step] = lax.ppermute(below, "rcv", up)
    by_shift[step] = lax.ppermute(above, "rcv", down)


def line_block(by_shift, flip):
    size = lax.axis_size("rcv")
    me = lax.axis_index("rcv")
    block = None
    for shift in sorted({(i ^ flip) - i for i in range(size)}):
        here = by_shift[shift]
        block = here if block is None else jnp.where((me ^ flip) - me == shift, here, block)
    return block


def src_gather(value, *others):
    size = lax.axis_size("src")
    got = {0: value}
    for flip in bits(size)[1:] + bits(size)[:1]:
        if flip == 1:
            got = after(got, *others)
        for key in list(got):
            got[key ^ flip] = swap(got[key], "src", flip)
    return [got[flip] for flip in range(size)]


def src_reduce(keep, send, flips):
    size = lax.axis_size("src")
    for flip in flips:
        total = keep + swap(send, "src", flip)
        half = total.shape[0] // 2
        if 2 * flip < size:
            keep, send = total[:half], total[half:]
    return (keep, send) if 2 * flips[-1] < size else total


def after(value, *others):
    return lax.optimization_barrier((value, *others))[0]


def estimate(flops, moved):
    return pl.CostEstimate(flops=int(flops), bytes_accessed=int(moved), transcendentals=0)


def whole(shape):
    return pl.BlockSpec(shape, lambda i: (0,) * len(shape))


def bin_kernel(n_block, n_piece, rows, tile_units, first, last, origin_ref, matrix_ref, *refs):
    sum_ref, refs = (None, refs) if first else (refs[0], refs[1:])
    n_flat = n_block * n_piece
    piece_refs, out_refs, both = refs[:n_flat], refs[n_flat:-1], refs[-1]
    length = piece_refs[0].shape[1]
    all_rows = n_piece * rows
    step = pl.program_id(0)

    @pl.when(step == 0)
    def _():
        for m in range(n_block):
            for q in range(n_piece):
                at, cols = reverse(q, n_piece) * rows, pl.ds(m * length, length)
                high, low = split(piece_refs[m * n_piece + q][:rows, :])
                both[pl.ds(at, rows), cols] = high
                both[pl.ds(all_rows + at, rows), cols] = low

    unit = matrix_ref.shape[0]
    out_refs = out_refs[0]
    wide = unit * tile_units
    total = None if first else sum_ref[...]
    wanted = lax.broadcasted_iota(jnp.int32, (wide, length), 0)
    for m in range(n_block):
        here = piece_refs[m * n_piece][rows : rows + 1, :].astype(jnp.int32)
        here = here - (origin_ref[0] + step * wide)
        hot = jnp.where(here == wanted, 1.0, 0.0).astype(jnp.bfloat16)
        term = dot(both[:, m * length : (m + 1) * length], hot, NT)
        term = term[:all_rows] + term[all_rows:]
        total = term if total is None else total + term
    if not last:
        out_refs[...] = total
        return
    half = rows // 2
    mat_high, mat_low = split(matrix_ref[...])
    for g in range(tile_units):
        sum_high, sum_low = split(total[:, g * unit : (g + 1) * unit])
        product = dot(jnp.concatenate([sum_high, sum_low], axis=0), mat_high, NN)
        product = product[:all_rows] + product[all_rows:] + dot(sum_high, mat_low, NN)
        cols = slice(g * LANES, (g + 1) * LANES)
        for q in range(n_piece):
            re, im = slice(q * rows, q * rows + half), slice(q * rows + half, (q + 1) * rows)
            for here, value in (
                (re, product[re, :LANES] - product[im, LANES:]),
                (im, product[re, LANES:] + product[im, :LANES]),
            ):
                if out_refs.dtype == jnp.float32:
                    out_refs[here, cols] = value
                else:
                    out_refs[0, here, cols], out_refs[1, here, cols] = split(value)


def bin_step(pieces, rows, origin, matrix, units, sums=(), last=True, halves=False):
    n_block, n_piece = len(pieces), len(pieces[0])
    length = pieces[0][0].shape[1]
    all_rows = n_piece * rows
    tile_units = min(4, units)
    tiles = units // tile_units
    width = matrix.shape[0] * tile_units
    lanes = LANES * tile_units
    tiled = lambda size: pl.BlockSpec((all_rows, size), lambda i: (0, i))
    if last and halves:
        out_spec = pl.BlockSpec((2, all_rows, lanes), lambda i: (0, 0, i))
        out_shape = jax.ShapeDtypeStruct((2, all_rows, tiles * lanes), jnp.bfloat16)
    else:
        size = lanes if last else width
        out_spec = tiled(size)
        out_shape = jax.ShapeDtypeStruct((all_rows, tiles * size), jnp.float32)
    flat = [piece for block in pieces for piece in block]
    return pl.pallas_call(
        functools.partial(bin_kernel, n_block, n_piece, rows, tile_units, not sums, last),
        grid=(tiles,),
        in_specs=[pl.BlockSpec(memory_space=pltpu.SMEM), whole(matrix.shape)]
        + [tiled(width) for _ in sums]
        + [whole(p.shape) for p in flat],
        out_specs=[out_spec],
        out_shape=[out_shape],
        scratch_shapes=[pltpu.VMEM((2 * all_rows, n_block * length), jnp.bfloat16)],
        compiler_params=pltpu.CompilerParams(vmem_limit_bytes=VMEM_LIMIT),
        cost_estimate=estimate(
            4 * all_rows * n_block * length * tiles * width, 4 * all_rows * tiles * width
        ),
        name="bin_traces",
    )(jnp.reshape(origin, (1,)).astype(jnp.int32), matrix, *sums, *flat)[0]


def multiply_kernel(n_piece, n_src, n_sum, order_ref, a_ref, *refs):
    x_refs, refs = refs[: max(1, n_piece)], refs[max(1, n_piece) :]
    sum_refs, out_refs = refs[:n_sum], refs[n_sum : n_sum + 2]
    if n_piece:
        both = refs[-1]
        rows, width = x_refs[0].shape

        @pl.when(pl.program_id(0) == 0)
        def _():
            for j in range(n_piece):
                number = reverse(j, n_piece)
                at = (reverse(number % n_src, n_src) ^ order_ref[0]) * rows
                at = pl.ds(pl.multiple_of(at, rows), rows)
                cols = ((number // n_src) ^ order_ref[1]) * width
                cols = pl.ds(pl.multiple_of(cols, width), width)
                both[0, at, cols], both[1, at, cols] = split(x_refs[j][...])
    else:
        both = x_refs[0]
        rows = both.shape[1] // n_src
    all_rows = n_src * rows
    high, stacked = both[0], both[...].reshape(2 * all_rows, both.shape[2])
    products = []
    for d in range(2):
        a_high, a_low = split(a_ref[d])
        wide = dot(stacked, a_high, NT)
        products.append(wide[:all_rows] + wide[all_rows:] + dot(high, a_low, NT))
    half = rows // 2
    for p in range(n_src):
        re, im = slice(p * rows, p * rows + half), slice(p * rows + half, (p + 1) * rows)
        at = p * rows % (all_rows // 2)
        out = p * rows // (all_rows // 2)
        for here, value in (
            (slice(at, at + half), products[0][re] - products[1][im]),
            (slice(at + half, at + rows), products[0][im] + products[1][re]),
        ):
            out_refs[out][here, :] = value if not n_sum else value + sum_refs[out][here, :]


def multiply(columns, order, aperture, depth_part=(0, 1), row_part=(0, 1), sums=(), sums_at=0):
    n_src = lax.axis_size("src")
    _, out_bins, depth = aperture.shape
    pieces = columns if isinstance(columns, list) else []
    depth, out_bins = depth // depth_part[1], out_bins // row_part[1]
    tile = min(512, out_bins)
    first = row_part[0] * (out_bins // tile)
    all_rows = n_src * pieces[0].shape[0] if pieces else columns.shape[1]
    inputs = pieces or [columns]
    out_spec = pl.BlockSpec((all_rows // 2, tile), lambda i: (0, i))
    out_shape = jax.ShapeDtypeStruct((all_rows // 2, out_bins), jnp.float32)
    return pl.pallas_call(
        functools.partial(multiply_kernel, len(pieces), n_src, len(sums)),
        grid=(out_bins // tile,),
        in_specs=[
            pl.BlockSpec(memory_space=pltpu.SMEM),
            pl.BlockSpec((2, tile, depth), lambda i: (0, first + i, depth_part[0])),
        ]
        + [whole(x.shape) for x in inputs]
        + [
            pl.BlockSpec((all_rows // 2, tile), lambda i: (0, sums_at * (out_bins // tile) + i))
            for _ in sums
        ],
        out_specs=[out_spec] * 2,
        out_shape=[out_shape] * 2,
        scratch_shapes=[pltpu.VMEM((2, all_rows, depth), jnp.bfloat16)] if pieces else [],
        compiler_params=pltpu.CompilerParams(vmem_limit_bytes=VMEM_LIMIT),
        cost_estimate=estimate(12 * all_rows * out_bins * depth, 8 * out_bins * depth),
        name="multiply",
    )(order, aperture, *inputs, *sums)


def spread(block, j):
    n_rcv, n_src = lax.axis_size("rcv"), lax.axis_size("src")
    fold = n_rcv // n_src
    pairs = [
        (r * n_src + s, (reverse((r % fold) * n_src + s, n_rcv) ^ j) * n_src + r // fold)
        for r in range(n_rcv)
        for s in range(n_src)
    ]
    return lax.ppermute(block, ("rcv", "src"), pairs)


def complex_product(left, right):
    return jnp.stack([left[0] * right[0] - left[1] * right[1], left[0] * right[1] + left[1] * right[0]])


def per_device(traces, moveout, trace_owner, trace_group, trace_table, aperture, shaping):
    n_rcv, n_src = lax.axis_size("rcv"), lax.axis_size("src")
    rcv, src = lax.axis_index("rcv"), lax.axis_index("src")
    fold = n_rcv // n_src
    shots, _, length = traces.shape
    _, tables, stencil = moveout.shape
    out_bins = aperture.shape[1]
    groups = out_bins // stencil
    rows = 2 * shots
    per_tile = LANES // stencil
    units = groups // per_tile

    parts = 2 if fold == 1 else 1
    quarters = parts
    part_bins = out_bins // parts

    code = ((trace_owner * groups + trace_group) * tables + trace_table).astype(jnp.float32)
    values = traces.transpose(1, 0, 2).reshape(rows, length)
    values = jnp.concatenate([values, jnp.broadcast_to(code, (8, length))], axis=0)
    matrix = jnp.einsum("ab,dkj->akdbj", jnp.eye(per_tile, dtype=jnp.float32), moveout,
                        precision=lax.Precision.HIGHEST)
    matrix = matrix.reshape(per_tile * tables, 2 * LANES)

    by_shift, blocks = {0: values}, [values]
    pieces = src_gather(values)
    origin = src * (fold * groups * tables)
    totals = []
    for m in range(n_rcv):
        if m + 1 < n_rcv:
            line_step(by_shift, m + 1, *totals[m - 2 : m - 1] if m > 1 else ())
            block = line_block(by_shift, m + 1)
            blocks.append(after(block, *totals[m - 1 : m] if m > 0 else ()))
            pieces = after(pieces, blocks[-1])
        last = m == n_rcv - 1
        totals.append(
            bin_step([pieces], rows, origin, matrix, fold * units, tuple(totals[-1:]), last, True)
        )
        if not last:
            pieces = src_gather(blocks[-1], totals[-1])
    columns = totals[-1]
    own = [[block] for block in blocks]
    shape_now = shaping.transpose(1, 0, 2)

    def bin_own(part, *others):
        place = after((rcv * parts + part) * (groups // parts * tables), *others)
        panel = bin_step(own, rows, place, matrix, units // parts)
        return panel.reshape(2, shots, part_bins)

    def subtract(part, mine, of):
        here = slice(part * out_bins // of, (part + 1) * out_bins // of)
        inner = slice((part * parts % of) * part_bins // of, (part * parts % of + parts) * part_bins // of)
        mine = mine.reshape(2, shots, out_bins // of)
        return binned[part * parts // of][:, :, inner] - complex_product(shape_now[:, :, here], mine)

    place = turn(rcv, n_rcv) ^ src
    turned = turn(place % n_src, n_src)
    order = jnp.stack([turned, place // n_src]).astype(jnp.int32)

    flips = bits(n_src)
    near, far = (flips[:1], flips[1:]) if n_src > 2 else ([], flips)
    half = n_rcv // 2
    binned, panels, received = [], [], []
    ready = order
    for h in range(parts):
        keep, send = multiply(columns, ready, aperture, (0, 1), (h, parts))
        if near:
            keep, send = src_reduce(keep, send, near)
        binned.append(bin_own(h, keep, *received[-1] if h else ()))
        if h:
            panel = after(panels[-1], keep)
            received[-1] += [spread(panel, j) for j in range(half, n_rcv)]
        mine = src_reduce(keep, send, far)
        if h:
            mine = after(mine, received[-1])
        panels.append(subtract(h, mine, parts).reshape(rows, part_bins))
        received.append([spread(panels[-1], j) for j in range(half)])
        ready = after(order, panels[-1])

    for sweep in range(1, ITERS):
        sums = []
        for c in range(parts - 1):
            for h in range(parts):
                ready = order
                if c == parts - 2 and h == 1:
                    received[-1] += [spread(after(panels[-1], sums[0]), j) for j in range(half, n_rcv)]
                    ready = after(order, received[-1][:half])
                fill = {"sums": sums[h], "sums_at": 0} if c else {}
                total = multiply(received[c], ready, aperture, (c, parts), (h, parts), **fill)
                sums[h:] = [total]
        if parts == 1:
            received[-1] += [spread(panels[-1], j) for j in range(half, n_rcv)]
        partial = []
        for h in range(quarters):
            fill = {} if parts == 1 else {"sums": sums[h * parts // quarters], "sums_at": h % (quarters // parts)}
            ready = after(order, partial[h - 1]) if h > 0 else order
            keep, send = multiply(received[-1], ready, aperture, (parts - 1, parts), (h, quarters), **fill)
            partial.append(src_reduce(keep, send, near) if near else (keep, send))
        panels = [subtract(h, src_reduce(*partial[h], far), quarters) for h in range(quarters)]
    return jnp.concatenate(panels, axis=2).transpose(1, 0, 2)


def solution(mesh):
    in_specs = (
        P(("freq", "src"), None, "rcv"),
        P(None, "freq", None),
        P(("freq", "rcv")),
        P(("freq", "rcv")),
        P(("freq", "rcv")),
        P(None, ("freq", "rcv"), "src"),
        P(("freq", "src"), None, "rcv"),
    )
    out_specs = P(("freq", "src"), None, "rcv")
    return jax.shard_map(
        per_device, mesh=mesh, in_specs=in_specs, out_specs=out_specs, check_vma=False
    )
```

time: 584 us -> 209 us (0.36)
  waiting for transfers between devices: 325 us -> 28.1 us
  matrix products: 146 us -> 0 us
  Pallas kernels: 0 us -> 104 us
  other arithmetic: 73.9 us -> 8.26 us
  starting transfers between devices: 0.65 us -> 59.3 us
  local copies, waits for them, and re-layouts: 23.4 us -> 8.45 us
  between operations: 13.6 us -> 0.55 us
    psum x2 -> x0, waiting for transfers between devices: 173 us -> none  [from_root(): return lax.psum(kept, axis)]
    dot_general x6 -> x0, matrix products: 145 us -> none  [the longest x4 79.2 us: interpolate(): jnp.einsum('sct,tdb->scdb', values, matrix, precision=lax.Precision.HIGHEST)]
    reduce_scatter x3 -> x0, waiting for transfers between devices: 106 us -> none  [the longest x2 59.7 us: multiply(): lax.psum_scatter(complex_join(jnp.einsum('sck,dik->scdi', columns, apertu...]
    pallas_call x0 -> x12, Pallas kernels: none -> 104 us  [the longest x6 52.9 us: multiply(): pl.pallas_call(functools.partial(multiply_kernel, len(pieces), n_src, len...]
    ppermute x0 -> x34, starting transfers between devices: none -> 59.3 us  [the longest x8 30.8 us: spread(): return lax.ppermute(block, ('rcv', 'src'), pairs)]
    mul x8 -> x0, other arithmetic: 51.8 us -> none  [the longest x4 48.9 us: bin_matrix(): matrix = group_hot[:, None, :, None] * weights[:, :, None, :]]
    all_gather x2 -> x0, waiting for transfers between devices: 46.2 us -> none  [to_columns(): shots_all = lax.all_gather(panel_now, 'src', axis=0, tiled=True)]
    ppermute x0 -> x34, waiting for transfers between devices: none -> 28.1 us  [the longest x20 13.2 us: swap(): return lax.ppermute(value, axis, [(i, i ^ flip) for i in range(size)])]
  transfers between devices with their start and end apart: 7 -> 34, of which waited for: 7 -> 12; matrix products, arithmetic and copies ran while one was open for 0% -> 3% of each run, Pallas kernels for 0% -> 27%
where the time goes in v2:
time: 209 us; the launch traced here: 208 us
  Pallas kernels  104 us (50%)
  starting transfers between devices  59.3 us (28%)
  waiting for transfers between devices  28.1 us (13%)
  local copies, waits for them, and re-layouts  8.45 us (4%)
  other arithmetic  8.26 us (4%)
    pallas_call x6, Pallas kernels, multiply(): pl.pallas_call(functools.partial(multiply_kernel, len(pieces), n_src, len...  52.9 us
    pallas_call x6, Pallas kernels, bin_step(): pl.pallas_call(functools.partial(bin_kernel, n_block, n_piece, rows, tile...  50.9 us
    ppermute x8, starting transfers between devices, spread(): return lax.ppermute(block, ('rcv', 'src'), pairs)  30.8 us
    ppermute x20, starting transfers between devices, swap(): return lax.ppermute(value, axis, [(i, i ^ flip) for i in range(size)])  18.5 us
    ppermute x20, waiting for transfers between devices, swap(): return lax.ppermute(value, axis, [(i, i ^ flip) for i in range(size)])  13.2 us
    ppermute x8, waiting for transfers between devices, spread(): return lax.ppermute(block, ('rcv', 'src'), pairs)  11.7 us
    ppermute x3, starting transfers between devices, line_step(): by_shift[-step] = lax.ppermute(below, 'rcv', up)  6.1 us
    unnamed x55, local copies, waits for them, and re-layouts  4.99 us
  transfers between devices with their start and end apart: 34, of which 12 were waited for; matrix products, arithmetic and copies ran while one was open for 3% of the time, Pallas kernels for 27%

profile of v2, /device:TPU:0, one launch (start us, length us, event | category | flops | bytes accessed | tf_op | source)
XLA Modules:
  0.0 208.5 jit_solution(17715772807567957354)
XLA Ops:
  0.0 1.0 copy.12
  1.8 3.0 %collective-permute-start = (f32[72,1024]{1,0:T(8,128)S(1)}, f32[72,1024]{1,0:T(8,128)S(1)}, u32[]{:S(2)}, u32[]{:S(2)}) collective-permute-start(f32[72,1024]{1,0:T(8,128)S(1)} %pad_maximum_fusion.refs_0_), channel_id=1, source_target_pairs={{0,2},{1,3},{2,0},{3,1},{4,6},{5,7},{6,4},{7,5},{8,10},{9,11},{10,... | collective-permute-start | bytes 884744 | tf_op jit(solution)/shard_map/ppermute | solution.py:44
  4.8 1.3 collective-permute-start.3
  6.1 4.6 %collective-permute-start.4 = (f32[72,1024]{1,0:T(8,128)S(1)}, f32[72,1024]{1,0:T(8,128)S(1)}, u32[]{:S(2)}, u32[]{:S(2)}) collective-permute-start(f32[72,1024]{1,0:T(8,128)S(1)} %pad_maximum_fusion.refs_0_), channel_id=1, source_target_pairs={{0,4},{4,8},{8,12},{1,5},{5,9},{9,13},{2,6},{6,10},{10,14},{3,7},{... | collective-permute-start | bytes 884744 | tf_op jit(solution)/shard_map/ppermute | solution.py:52
  10.7 1.1 collective-permute-done.refs_2_
  12.3 0.9 multiply_bitcast_fusion
  13.5 0.8 copy.16.matrix_ref
  14.4 0.8 collective-permute-done.3
  15.2 1.2 collective-permute-done.4
  16.4 1.3 collective-permute-start.8
  19.6 7.8 %bin_traces.6.refs_0_ = f32[256,4096]{1,0:T(8,128)} custom-call(s32[1]{0:T(128)} %bitcast.2.origin_ref, f32[256,256]{1,0:T(8,128)} %copy.16.matrix_ref, f32[72,1024]{1,0:T(8,128)} %copy-done.14, f32[72,1024]{1,0:T(8,128)} %copy-done.20, f32[72,1024]{1,0:T(8,128)} %copy-done.19, f32[72,1024]{1,0:T(8,128)} %copy-done.22), custom_call_target="tpu_custom_call" | custom-call | flops 4294967296 | bytes 4194304 | tf_op jit(solution)/shard_map/bin_traces/pallas_call | solution.py:167
  28.1 1.3 collective-permute-start.13
  29.4 0.9 collective-permute-start.14
  30.2 1.7 collective-permute-start.10
  32.7 8.5 %bin_traces.7.refs_0_ = f32[256,4096]{1,0:T(8,128)} custom-call(s32[1]{0:T(128)} %bitcast.2.origin_ref, f32[256,256]{1,0:T(8,128)} %copy.16.matrix_ref, f32[256,4096]{1,0:T(8,128)} %bin_traces.6.refs_0_, f32[72,1024]{1,0:T(8,128)} %copy-done.12, f32[72,1024]{1,0:T(8,128)} %copy-done.25, f32[72,1024]{1,0:T(8,128)} %copy-done.23, ...), custom_call_target="tpu_custom_call" | custom-call | flops 4294967296 | bytes 4194304 | tf_op jit(solution)/shard_map/bin_traces/pallas_call | solution.py:167
  41.7 1.3 collective-permute-done.13
  43.0 1.7 collective-permute-start.15
  46.2 8.4 %bin_traces.8.refs_0_ = f32[256,4096]{1,0:T(8,128)} custom-call(s32[1]{0:T(128)} %bitcast.2.origin_ref, f32[256,256]{1,0:T(8,128)} %copy.16.matrix_ref, f32[256,4096]{1,0:T(8,128)} %bin_traces.7.refs_0_, f32[72,1024]{1,0:T(8,128)} %copy-done.13, f32[72,1024]{1,0:T(8,128)} %copy-done.24, f32[72,1024]{1,0:T(8,128)} %copy-done.21, f32[72,1024]{1,0:T(8,128)} %copy-done.26), custom_call_target="tpu_custom_call" | custom-call | flops 4294967296 | bytes 4194304 | tf_op jit(solution)/shard_map/bin_traces/pallas_call | solution.py:167
  57.7 9.6 %bin_traces.9.refs_0_ = bf16[2,256,2048]{2,1,0:T(8,128)(2,1)} custom-call(s32[1]{0:T(128)} %bitcast.2.origin_ref, f32[256,256]{1,0:T(8,128)} %copy.16.matrix_ref, f32[256,4096]{1,0:T(8,128)} %bin_traces.8.refs_0_, f32[72,1024]{1,0:T(8,128)} %copy-done.15, f32[72,1024]{1,0:T(8,128)} %copy-done.17, f32[72,1024]{1,0:T(8,128)} %copy-done.16, f32[72,1024]{1,0:T(8,128)} %copy-done.18), custom_call_target="tpu_custom_call" | custom-call | flops 4294967296 | bytes 4194304 | tf_op jit(solution)/shard_map/bin_traces/pallas_call | solution.py:167
  67.3 11.8 %multiply.9 = (f32[128,1024]{1,0:T(8,128)}, f32[128,1024]{1,0:T(8,128)}) custom-call(s32[2]{0:T(128)} %pad_add_fusion.order_ref, f32[2,2048,2048]{2,1,0:T(8,128)} %a_ref.11, bf16[2,256,2048]{2,1,0:T(8,128)(2,1)} %bin_traces.9.refs_0_), custom_call_target="tpu_custom_call" | custom-call | flops 6442450944 | bytes 16777216 | tf_op jit(solution)/shard_map/multiply/pallas_call | solution.py:233
  79.2 2.0 collective-permute-done.18
  81.2 1.1 add.61
  83.1 8.3 %bin_traces.10 = f32[64,1024]{1,0:T(8,128)} custom-call(s32[1]{0:T(128)} %bitcast.6.origin_ref, f32[256,256]{1,0:T(8,128)} %copy.16.matrix_ref, f32[72,1024]{1,0:T(8,128)} %copy-done.14, f32[72,1024]{1,0:T(8,128)} %copy-done.12, f32[72,1024]{1,0:T(8,128)} %copy-done.13, f32[72,1024]{1,0:T(8,128)} %copy-done.15), custom_call_target="tpu_custom_call" | custom-call | flops 2147483648 | bytes 524288 | tf_op jit(solution)/shard_map/bin_traces/pallas_call | solution.py:167
  91.5 1.0 bitcast_subtract_fusion.1
  92.5 12.0 %multiply.10 = (f32[128,1024]{1,0:T(8,128)}, f32[128,1024]{1,0:T(8,128)}) custom-call(s32[2]{0:T(128)} %pad_add_fusion.order_ref, f32[2,2048,2048]{2,1,0:T(8,128)} %a_ref.11, bf16[2,256,2048]{2,1,0:T(8,128)(2,1)} %bin_traces.9.refs_0_), custom_call_target="tpu_custom_call" | custom-call | flops 6442450944 | bytes 16777216 | tf_op jit(solution)/shard_map/multiply/pallas_call | solution.py:233
  105.2 6.4 %collective-permute-start.22 = (f32[64,1024]{1,0:T(8,128)S(1)}, f32[64,1024]{1,0:T(8,128)S(1)}, u32[]{:S(2)}, u32[]{:S(2)}) collective-permute-start(f32[64,1024]{1,0:T(8,128)S(1)} %bitcast_subtract_fusion.1), channel_id=1, source_target_pairs={{0,4},{1,12},{2,0},{3,8},{4,5},{5,13},{6,1},{7,9},{8,6},{9,14},{10... | collective-permute-start | bytes 786440 | tf_op jit(solution)/shard_map/ppermute | solution.py:262
  111.7 1.1 add.65
  112.8 1.5 collective-permute-start.23
  114.4 2.9 %collective-permute-start.24 = (f32[64,1024]{1,0:T(8,128)S(1)}, f32[64,1024]{1,0:T(8,128)S(1)}, u32[]{:S(2)}, u32[]{:S(2)}) collective-permute-start(f32[64,1024]{1,0:T(8,128)S(1)} %bitcast_subtract_fusion.1), channel_id=1, source_target_pairs={{0,8},{1,0},{2,12},{3,4},{4,9},{5,1},{6,13},{7,5},{8,10},{9,2},{10... | collective-permute-start | bytes 786440 | tf_op jit(solution)/shard_map/ppermute | solution.py:262
  117.3 3.3 %collective-permute-start.25 = (f32[64,1024]{1,0:T(8,128)S(1)}, f32[64,1024]{1,0:T(8,128)S(1)}, u32[]{:S(2)}, u32[]{:S(2)}) collective-permute-start(f32[64,1024]{1,0:T(8,128)S(1)} %bitcast_subtract_fusion.1), channel_id=1, source_target_pairs={{0,12},{1,4},{2,8},{3,0},{4,13},{5,5},{6,9},{7,1},{8,14},{9,6},{10... | collective-permute-start | bytes 786440 | tf_op jit(solution)/shard_map/ppermute | solution.py:262
  120.5 4.2 %collective-permute-done.22.refs_1_ = f32[64,1024]{1,0:T(8,128)S(1)} collective-permute-done((f32[64,1024]{1,0:T(8,128)S(1)}, f32[64,1024]{1,0:T(8,128)S(1)}, u32[]{:S(2)}, u32[]{:S(2)}) %collective-permute-start.22) | collective-permute-done | bytes 262176 | tf_op jit(solution)/shard_map/ppermute | solution.py:262
  124.8 8.4 %bin_traces.11 = f32[64,1024]{1,0:T(8,128)} custom-call(s32[1]{0:T(128)} %bitcast.14.origin_ref, f32[256,256]{1,0:T(8,128)} %copy.16.matrix_ref, f32[72,1024]{1,0:T(8,128)} %copy-done.14, f32[72,1024]{1,0:T(8,128)} %copy-done.12, f32[72,1024]{1,0:T(8,128)} %copy-done.13, f32[72,1024]{1,0:T(8,128)} %copy-done.15), custom_call_target="tpu_custom_call" | custom-call | flops 2147483648 | bytes 524288 | tf_op jit(solution)/shard_map/bin_traces/pallas_call | solution.py:167
  133.3 1.1 bitcast_subtract_fusion
  135.1 6.3 %collective-permute-start.27 = (f32[64,1024]{1,0:T(8,128)S(1)}, f32[64,1024]{1,0:T(8,128)S(1)}, u32[]{:S(2)}, u32[]{:S(2)}) collective-permute-start(f32[64,1024]{1,0:T(8,128)S(1)} %bitcast_subtract_fusion), channel_id=1, source_target_pairs={{0,4},{1,12},{2,0},{3,8},{4,5},{5,13},{6,1},{7,9},{8,6},{9,14},{10... | collective-permute-start | bytes 786440 | tf_op jit(solution)/shard_map/ppermute | solution.py:262
  141.4 7.2 %multiply.11 = (f32[128,1024]{1,0:T(8,128)}, f32[128,1024]{1,0:T(8,128)}) custom-call(s32[2]{0:T(128)} %pad_add_fusion.order_ref, f32[2,2048,2048]{2,1,0:T(8,128)} %a_ref.11, f32[64,1024]{1,0:T(8,128)} %copy-done, f32[64,1024]{1,0:T(8,128)} %copy-done.1, f32[64,1024]{1,0:T(8,128)} %copy-done.2, f32[64,1024]{1,0:T(8,128)} %copy-done.3), custom_call_target="tpu_custom_call" | custom-call | flops 3221225472 | bytes 8388608 | tf_op jit(solution)/shard_map/multiply/pallas_call | solution.py:233
  148.5 8.5 %collective-permute-start.28 = (f32[64,1024]{1,0:T(8,128)S(1)}, f32[64,1024]{1,0:T(8,128)S(1)}, u32[]{:S(2)}, u32[]{:S(2)}) collective-permute-start(f32[64,1024]{1,0:T(8,128)S(1)} %bitcast_subtract_fusion), channel_id=1, source_target_pairs={{0,8},{1,0},{2,12},{3,4},{4,9},{5,1},{6,13},{7,5},{8,10},{9,2},{10... | collective-permute-start | bytes 786440 | tf_op jit(solution)/shard_map/ppermute | solution.py:262
  157.1 2.0 collective-permute-start.29
  159.1 4.6 %collective-permute-done.28.refs_2_ = f32[64,1024]{1,0:T(8,128)S(1)} collective-permute-done((f32[64,1024]{1,0:T(8,128)S(1)}, f32[64,1024]{1,0:T(8,128)S(1)}, u32[]{:S(2)}, u32[]{:S(2)}) %collective-permute-start.28) | collective-permute-done | bytes 262176 | tf_op jit(solution)/shard_map/ppermute | solution.py:262
  163.7 2.9 %collective-permute-done.29.refs_3_ = f32[64,1024]{1,0:T(8,128)S(1)} collective-permute-done((f32[64,1024]{1,0:T(8,128)S(1)}, f32[64,1024]{1,0:T(8,128)S(1)}, u32[]{:S(2)}, u32[]{:S(2)}) %collective-permute-start.29) | collective-permute-done | bytes 262176 | tf_op jit(solution)/shard_map/ppermute | solution.py:262
  167.3 7.3 %multiply.12 = (f32[128,1024]{1,0:T(8,128)}, f32[128,1024]{1,0:T(8,128)}) custom-call(s32[2]{0:T(128)} %pad_add_fusion.order_ref, f32[2,2048,2048]{2,1,0:T(8,128)} %a_ref.11, f32[64,1024]{1,0:T(8,128)} %copy-done.4, f32[64,1024]{1,0:T(8,128)} %copy-done.5, f32[64,1024]{1,0:T(8,128)} %copy-done.6, f32[64,1024]{1,0:T(8,128)} %copy-done.7, ...), custom_call_target="tpu_custom_call" | custom-call | flops 3221225472 | bytes 8388608 | tf_op jit(solution)/shard_map/multiply/pallas_call | solution.py:233
  174.6 7.3 %multiply.13 = (f32[128,1024]{1,0:T(8,128)}, f32[128,1024]{1,0:T(8,128)}) custom-call(s32[2]{0:T(128)} %pad_add_fusion.order_ref, f32[2,2048,2048]{2,1,0:T(8,128)} %a_ref.11, f32[64,1024]{1,0:T(8,128)} %copy-done, f32[64,1024]{1,0:T(8,128)} %copy-done.1, f32[64,1024]{1,0:T(8,128)} %copy-done.2, f32[64,1024]{1,0:T(8,128)} %copy-done.3), custom_call_target="tpu_custom_call" | custom-call | flops 3221225472 | bytes 8388608 | tf_op jit(solution)/shard_map/multiply/pallas_call | solution.py:233
  182.0 7.4 %multiply.14 = (f32[128,1024]{1,0:T(8,128)}, f32[128,1024]{1,0:T(8,128)}) custom-call(s32[2]{0:T(128)} %pad_add_fusion.order_ref, f32[2,2048,2048]{2,1,0:T(8,128)} %a_ref.11, f32[64,1024]{1,0:T(8,128)} %copy-done.4, f32[64,1024]{1,0:T(8,128)} %copy-done.5, f32[64,1024]{1,0:T(8,128)} %copy-done.6, f32[64,1024]{1,0:T(8,128)} %copy-done.7, ...), custom_call_target="tpu_custom_call" | custom-call | flops 3221225472 | bytes 8388608 | tf_op jit(solution)/shard_map/multiply/pallas_call | solution.py:233
  190.0 4.9 %collective-permute-start.31 = (f32[64,1024]{1,0:T(8,128)S(1)}, f32[64,1024]{1,0:T(8,128)S(1)}, u32[]{:S(2)}, u32[]{:S(2)}) collective-permute-start(f32[64,1024]{1,0:T(8,128)S(1)} %slice.127), channel_id=1, source_target_pairs={{0,2},{1,3},{2,0},{3,1},{4,6},{5,7},{6,4},{7,5},{8,10},{9,11},{10,... | collective-permute-start | bytes 786440 | tf_op jit(solution)/shard_map/ppermute | solution.py:44
  194.9 1.1 add.71
  196.0 1.8 collective-permute-start.33
  197.8 4.1 %collective-permute-done.31 = f32[64,1024]{1,0:T(8,128)S(1)} collective-permute-done((f32[64,1024]{1,0:T(8,128)S(1)}, f32[64,1024]{1,0:T(8,128)S(1)}, u32[]{:S(2)}, u32[]{:S(2)}) %collective-permute-start.31) | collective-permute-done | bytes 262176 | tf_op jit(solution)/shard_map/ppermute | solution.py:44
  202.0 5.0 %collective-permute-done.33 = f32[64,1024]{1,0:T(8,128)S(1)} collective-permute-done((f32[64,1024]{1,0:T(8,128)S(1)}, f32[64,1024]{1,0:T(8,128)S(1)}, u32[]{:S(2)}, u32[]{:S(2)}) %collective-permute-start.33) | collective-permute-done | bytes 262176 | tf_op jit(solution)/shard_map/ppermute | solution.py:44
  207.3 1.2 copy.20
  (121 shorter events, 14.1 us)
Async XLA Ops:
  1.8 17.0 %copy-start.14 = (f32[72,1024]{1,0:T(8,128)}, f32[72,1024]{1,0:T(8,128)S(1)}, u32[]{:S(2)}) copy-start(f32[72,1024]{1,0:T(8,128)S(1)} %pad_maximum_fusion.refs_0_) | copy-start | bytes 884740
  1.8 10.0 %collective-permute-start = (f32[72,1024]{1,0:T(8,128)S(1)}, f32[72,1024]{1,0:T(8,128)S(1)}, u32[]{:S(2)}, u32[]{:S(2)}) collective-permute-start(f32[72,1024]{1,0:T(8,128)S(1)} %pad_maximum_fusion.refs_0_), channel_id=1, source_target_pairs={{0,2},{1,3},{2,0},{3,1},{4,6},{5,7},{6,4},{7,5},{8,10},{9,11},{10,... | collective-permute-start | bytes 884744 | tf_op jit(solution)/shard_map/ppermute | solution.py:44
  4.8 10.3 %collective-permute-start.3 = (f32[72,1024]{1,0:T(8,128)S(1)}, f32[72,1024]{1,0:T(8,128)S(1)}, u32[]{:S(2)}, u32[]{:S(2)}) collective-permute-start(f32[72,1024]{1,0:T(8,128)S(1)} %pad_maximum_fusion.refs_0_), channel_id=1, source_target_pairs={{4,0},{8,4},{12,8},{5,1},{9,5},{13,9},{6,2},{10,6},{14,10},{7,3},{... | collective-permute-start | bytes 884744 | tf_op jit(solution)/shard_map/ppermute | solution.py:53
  6.1 10.2 %collective-permute-start.4 = (f32[72,1024]{1,0:T(8,128)S(1)}, f32[72,1024]{1,0:T(8,128)S(1)}, u32[]{:S(2)}, u32[]{:S(2)}) collective-permute-start(f32[72,1024]{1,0:T(8,128)S(1)} %pad_maximum_fusion.refs_0_), channel_id=1, source_target_pairs={{0,4},{4,8},{8,12},{1,5},{5,9},{9,13},{2,6},{6,10},{10,14},{3,7},{... | collective-permute-start | bytes 884744 | tf_op jit(solution)/shard_map/ppermute | solution.py:52
  11.8 7.0 %collective-permute-start.1 = (f32[72,1024]{1,0:T(8,128)S(1)}, f32[72,1024]{1,0:T(8,128)S(1)}, u32[]{:S(2)}, u32[]{:S(2)}) collective-permute-start(f32[72,1024]{1,0:T(8,128)S(1)} %pad_maximum_fusion.refs_0_), channel_id=1, source_target_pairs={{0,1},{1,0},{2,3},{3,2},{4,5},{5,4},{6,7},{7,6},{8,9},{9,8},{10,11... | collective-permute-start | bytes 884744 | tf_op jit(solution)/shard_map/ppermute | solution.py:44
  11.8 7.0 %collective-permute-start.2 = (f32[72,1024]{1,0:T(8,128)S(1)}, f32[72,1024]{1,0:T(8,128)S(1)}, u32[]{:S(2)}, u32[]{:S(2)}) collective-permute-start(f32[72,1024]{1,0:T(8,128)S(1)} %collective-permute-done.refs_2_), channel_id=1, source_target_pairs={{0,1},{1,0},{2,3},{3,2},{4,5},{5,4},{6,7},{7,6},{8,9},{9,8},{10,11... | collective-permute-start | bytes 884744 | tf_op jit(solution)/shard_map/ppermute | solution.py:44
  16.4 11.0 %copy-start.12 = (f32[72,1024]{1,0:T(8,128)}, f32[72,1024]{1,0:T(8,128)S(1)}, u32[]{:S(2)}) copy-start(f32[72,1024]{1,0:T(8,128)S(1)} %broadcast_select_fusion.1.refs_1_) | copy-start | bytes 884740
  16.4 11.6 %collective-permute-start.8 = (f32[72,1024]{1,0:T(8,128)S(1)}, f32[72,1024]{1,0:T(8,128)S(1)}, u32[]{:S(2)}, u32[]{:S(2)}) collective-permute-start(f32[72,1024]{1,0:T(8,128)S(1)} %collective-permute-done.3), channel_id=1, source_target_pairs={{4,0},{8,4},{5,1},{9,5},{6,2},{10,6},{7,3},{11,7},{20,16},{24,20},... | collective-permute-start | bytes 884744 | tf_op jit(solution)/shard_map/ppermute | solution.py:53
  17.7 10.3 %collective-permute-start.9 = (f32[72,1024]{1,0:T(8,128)S(1)}, f32[72,1024]{1,0:T(8,128)S(1)}, u32[]{:S(2)}, u32[]{:S(2)}) collective-permute-start(f32[72,1024]{1,0:T(8,128)S(1)} %collective-permute-done.4), channel_id=1, source_target_pairs={{4,8},{8,12},{5,9},{9,13},{6,10},{10,14},{7,11},{11,15},{20,24},{2... | collective-permute-start | bytes 884744 | tf_op jit(solution)/shard_map/ppermute | solution.py:52
  18.4 9.0 %collective-permute-start.5 = (f32[72,1024]{1,0:T(8,128)S(1)}, f32[72,1024]{1,0:T(8,128)S(1)}, u32[]{:S(2)}, u32[]{:S(2)}) collective-permute-start(f32[72,1024]{1,0:T(8,128)S(1)} %broadcast_select_fusion.1.refs_1_), channel_id=1, source_target_pairs={{0,2},{1,3},{2,0},{3,1},{4,6},{5,7},{6,4},{7,5},{8,10},{9,11},{10,... | collective-permute-start | bytes 884744 | tf_op jit(solution)/shard_map/ppermute | solution.py:44
  27.4 4.5 %collective-permute-start.6 = (f32[72,1024]{1,0:T(8,128)S(1)}, f32[72,1024]{1,0:T(8,128)S(1)}, u32[]{:S(2)}, u32[]{:S(2)}) collective-permute-start(f32[72,1024]{1,0:T(8,128)S(1)} %broadcast_select_fusion.1.refs_1_), channel_id=1, source_target_pairs={{0,1},{1,0},{2,3},{3,2},{4,5},{5,4},{6,7},{7,6},{8,9},{9,8},{10,11... | collective-permute-start | bytes 884744 | tf_op jit(solution)/shard_map/ppermute | solution.py:44
  27.5 4.4 %collective-permute-start.7 = (f32[72,1024]{1,0:T(8,128)S(1)}, f32[72,1024]{1,0:T(8,128)}, u32[]{:S(2)}, u32[]{:S(2)}) collective-permute-start(f32[72,1024]{1,0:T(8,128)S(1)} %collective-permute-done.5.refs_3_), channel_id=1, source_target_pairs={{0,1},{1,0},{2,3},{3,2},{4,5},{5,4},{6,7},{7,6},{8,9},{9,8},{10,11... | collective-permute-start | bytes 884744 | tf_op jit(solution)/shard_map/ppermute | solution.py:44
  28.0 13.1 %copy-start.13 = (f32[72,1024]{1,0:T(8,128)}, f32[72,1024]{1,0:T(8,128)S(1)}, u32[]{:S(2)}) copy-start(f32[72,1024]{1,0:T(8,128)S(1)} %broadcast_select_fusion.refs_1_.refs_2_) | copy-start | bytes 884740
  28.1 14.9 %collective-permute-start.13 = (f32[72,1024]{1,0:T(8,128)S(1)}, f32[72,1024]{1,0:T(8,128)S(1)}, u32[]{:S(2)}, u32[]{:S(2)}) collective-permute-start(f32[72,1024]{1,0:T(8,128)S(1)} %collective-permute-done.8), channel_id=1, source_target_pairs={{4,0},{5,1},{6,2},{7,3},{20,16},{21,17},{22,18},{23,19}} | collective-permute-start | bytes 884744 | tf_op jit(solution)/shard_map/ppermute | solution.py:53
  29.4 13.6 %collective-permute-start.14 = (f32[72,1024]{1,0:T(8,128)S(1)}, f32[72,1024]{1,0:T(8,128)S(1)}, u32[]{:S(2)}, u32[]{:S(2)}) collective-permute-start(f32[72,1024]{1,0:T(8,128)S(1)} %collective-permute-done.9), channel_id=1, source_target_pairs={{8,12},{9,13},{10,14},{11,15},{24,28},{25,29},{26,30},{27,31}} | collective-permute-start | bytes 884744 | tf_op jit(solution)/shard_map/ppermute | solution.py:52
  30.2 10.9 %collective-permute-start.10 = (f32[72,1024]{1,0:T(8,128)S(1)}, f32[72,1024]{1,0:T(8,128)S(1)}, u32[]{:S(2)}, u32[]{:S(2)}) collective-permute-start(f32[72,1024]{1,0:T(8,128)S(1)} %broadcast_select_fusion.refs_1_.refs_2_), channel_id=1, source_target_pairs={{0,2},{1,3},{2,0},{3,1},{4,6},{5,7},{6,4},{7,5},{8,10},{9,11},{10,... | collective-permute-start | bytes 884744 | tf_op jit(solution)/shard_map/ppermute | solution.py:44
  41.1 3.6 %collective-permute-start.11 = (f32[72,1024]{1,0:T(8,128)S(1)}, f32[72,1024]{1,0:T(8,128)S(1)}, u32[]{:S(2)}, u32[]{:S(2)}) collective-permute-start(f32[72,1024]{1,0:T(8,128)S(1)} %broadcast_select_fusion.refs_1_.refs_2_), channel_id=1, source_target_pairs={{0,1},{1,0},{2,3},{3,2},{4,5},{5,4},{6,7},{7,6},{8,9},{9,8},{10,11... | collective-permute-start | bytes 884744 | tf_op jit(solution)/shard_map/ppermute | solution.py:44
  41.2 3.6 %collective-permute-start.12 = (f32[72,1024]{1,0:T(8,128)S(1)}, f32[72,1024]{1,0:T(8,128)S(1)}, u32[]{:S(2)}, u32[]{:S(2)}) collective-permute-start(f32[72,1024]{1,0:T(8,128)S(1)} %collective-permute-done.10.refs_3_), channel_id=1, source_target_pairs={{0,1},{1,0},{2,3},{3,2},{4,5},{5,4},{6,7},{7,6},{8,9},{9,8},{10,11... | collective-permute-start | bytes 884744 | tf_op jit(solution)/shard_map/ppermute | solution.py:44
  43.0 11.6 %copy-start.15 = (f32[72,1024]{1,0:T(8,128)}, f32[72,1024]{1,0:T(8,128)S(1)}, u32[]{:S(2)}) copy-start(f32[72,1024]{1,0:T(8,128)S(1)} %select_select_fusion.refs_1_.refs_3_) | copy-start | bytes 884740
  43.0 11.6 %collective-permute-start.15 = (f32[72,1024]{1,0:T(8,128)S(1)}, f32[72,1024]{1,0:T(8,128)S(1)}, u32[]{:S(2)}, u32[]{:S(2)}) collective-permute-start(f32[72,1024]{1,0:T(8,128)S(1)} %select_select_fusion.refs_1_.refs_3_), channel_id=1, source_target_pairs={{0,2},{1,3},{2,0},{3,1},{4,6},{5,7},{6,4},{7,5},{8,10},{9,11},{10,... | collective-permute-start | bytes 884744 | tf_op jit(solution)/shard_map/ppermute | solution.py:44
  54.7 1.6 collective-permute-start.16
  54.7 2.0 collective-permute-start.17
  67.3 15.5 %copy-start.11 = (f32[32,2,2048]{2,1,0:T(2,128)S(1)}, f32[32,2,2048]{2,1,0:T(2,128)}, u32[]{:S(2)}) copy-start(f32[32,2,2048]{2,1,0:T(2,128)} %param.13) | copy-start | bytes 1572868
  79.1 2.1 %collective-permute-start.18 = (f32[128,1024]{1,0:T(8,128)}, f32[128,1024]{1,0:T(8,128)S(1)}, u32[]{:S(2)}, u32[]{:S(2)}) collective-permute-start(f32[128,1024]{1,0:T(8,128)} %get-tuple-element.82), channel_id=1, source_target_pairs={{0,1},{1,0},{2,3},{3,2},{4,5},{5,4},{6,7},{7,6},{8,9},{9,8},{10,11... | collective-permute-start | bytes 1572872 | tf_op jit(solution)/shard_map/ppermute | solution.py:44
  82.3 9.1 %collective-permute-start.19 = (f32[64,1024]{1,0:T(8,128)S(1)}, f32[64,1024]{1,0:T(8,128)S(1)}, u32[]{:S(2)}, u32[]{:S(2)}) collective-permute-start(f32[64,1024]{1,0:T(8,128)S(1)} %slice.118), channel_id=1, source_target_pairs={{0,2},{1,3},{2,0},{3,1},{4,6},{5,7},{6,4},{7,5},{8,10},{9,11},{10,... | collective-permute-start | bytes 786440 | tf_op jit(solution)/shard_map/ppermute | solution.py:44
  104.5 7.1 %collective-permute-start.20 = (f32[128,1024]{1,0:T(8,128)}, f32[128,1024]{1,0:T(8,128)S(1)}, u32[]{:S(2)}, u32[]{:S(2)}) collective-permute-start(f32[128,1024]{1,0:T(8,128)} %get-tuple-element.86), channel_id=1, source_target_pairs={{0,1},{1,0},{2,3},{3,2},{4,5},{5,4},{6,7},{7,6},{8,9},{9,8},{10,11... | collective-permute-start | bytes 1572872 | tf_op jit(solution)/shard_map/ppermute | solution.py:44
  104.5 16.0 %collective-permute-start.21 = (f32[64,1024]{1,0:T(8,128)S(1)}, f32[64,1024]{1,0:T(8,128)S(1)}, u32[]{:S(2)}, u32[]{:S(2)}) collective-permute-start(f32[64,1024]{1,0:T(8,128)S(1)} %bitcast_subtract_fusion.1), channel_id=1, source_target_pairs={{0,0},{1,8},{2,4},{3,12},{4,1},{5,9},{6,5},{7,13},{8,2},{9,10},{10... | collective-permute-start | bytes 786440 | tf_op jit(solution)/shard_map/ppermute | solution.py:262
  105.2 19.6 %collective-permute-start.22 = (f32[64,1024]{1,0:T(8,128)S(1)}, f32[64,1024]{1,0:T(8,128)S(1)}, u32[]{:S(2)}, u32[]{:S(2)}) collective-permute-start(f32[64,1024]{1,0:T(8,128)S(1)} %bitcast_subtract_fusion.1), channel_id=1, source_target_pairs={{0,4},{1,12},{2,0},{3,8},{4,5},{5,13},{6,1},{7,9},{8,6},{9,14},{10... | collective-permute-start | bytes 786440 | tf_op jit(solution)/shard_map/ppermute | solution.py:262
  112.8 20.3 %collective-permute-start.23 = (f32[64,1024]{1,0:T(8,128)S(1)}, f32[64,1024]{1,0:T(8,128)S(1)}, u32[]{:S(2)}, u32[]{:S(2)}) collective-permute-start(f32[64,1024]{1,0:T(8,128)S(1)} %slice.124), channel_id=1, source_target_pairs={{0,2},{1,3},{2,0},{3,1},{4,6},{5,7},{6,4},{7,5},{8,10},{9,11},{10,... | collective-permute-start | bytes 786440 | tf_op jit(solution)/shard_map/ppermute | solution.py:44
  114.4 18.9 %collective-permute-start.24 = (f32[64,1024]{1,0:T(8,128)S(1)}, f32[64,1024]{1,0:T(8,128)S(1)}, u32[]{:S(2)}, u32[]{:S(2)}) collective-permute-start(f32[64,1024]{1,0:T(8,128)S(1)} %bitcast_subtract_fusion.1), channel_id=1, source_target_pairs={{0,8},{1,0},{2,12},{3,4},{4,9},{5,1},{6,13},{7,5},{8,10},{9,2},{10... | collective-permute-start | bytes 786440 | tf_op jit(solution)/shard_map/ppermute | solution.py:262
  117.3 16.0 %collective-permute-start.25 = (f32[64,1024]{1,0:T(8,128)S(1)}, f32[64,1024]{1,0:T(8,128)S(1)}, u32[]{:S(2)}, u32[]{:S(2)}) collective-permute-start(f32[64,1024]{1,0:T(8,128)S(1)} %bitcast_subtract_fusion.1), channel_id=1, source_target_pairs={{0,12},{1,4},{2,8},{3,0},{4,13},{5,5},{6,9},{7,1},{8,14},{9,6},{10... | collective-permute-start | bytes 786440 | tf_op jit(solution)/shard_map/ppermute | solution.py:262
  120.5 12.7 %copy-start = (f32[64,1024]{1,0:T(8,128)}, f32[64,1024]{1,0:T(8,128)S(1)}, u32[]{:S(2)}) copy-start(f32[64,1024]{1,0:T(8,128)S(1)} %collective-permute-done.21.refs_0_) | copy-start | bytes 786436
  124.8 8.4 %copy-start.1 = (f32[64,1024]{1,0:T(8,128)}, f32[64,1024]{1,0:T(8,128)S(1)}, u32[]{:S(2)}) copy-start(f32[64,1024]{1,0:T(8,128)S(1)} %collective-permute-done.22.refs_1_) | copy-start | bytes 786436
  133.2 8.1 %copy-start.2 = (f32[64,1024]{1,0:T(8,128)}, f32[64,1024]{1,0:T(8,128)S(1)}, u32[]{:S(2)}) copy-start(f32[64,1024]{1,0:T(8,128)S(1)} %collective-permute-done.24.refs_2_) | copy-start | bytes 786436
  133.2 8.1 %copy-start.3 = (f32[64,1024]{1,0:T(8,128)}, f32[64,1024]{1,0:T(8,128)S(1)}, u32[]{:S(2)}) copy-start(f32[64,1024]{1,0:T(8,128)S(1)} %collective-permute-done.25.refs_3_) | copy-start | bytes 786436
  134.4 24.7 %collective-permute-start.26 = (f32[64,1024]{1,0:T(8,128)S(1)}, f32[64,1024]{1,0:T(8,128)S(1)}, u32[]{:S(2)}, u32[]{:S(2)}) collective-permute-start(f32[64,1024]{1,0:T(8,128)S(1)} %bitcast_subtract_fusion), channel_id=1, source_target_pairs={{0,0},{1,8},{2,4},{3,12},{4,1},{5,9},{6,5},{7,13},{8,2},{9,10},{10... | collective-permute-start | bytes 786440 | tf_op jit(solution)/shard_map/ppermute | solution.py:262
  135.1 24.0 %collective-permute-start.27 = (f32[64,1024]{1,0:T(8,128)S(1)}, f32[64,1024]{1,0:T(8,128)S(1)}, u32[]{:S(2)}, u32[]{:S(2)}) collective-permute-start(f32[64,1024]{1,0:T(8,128)S(1)} %bitcast_subtract_fusion), channel_id=1, source_target_pairs={{0,4},{1,12},{2,0},{3,8},{4,5},{5,13},{6,1},{7,9},{8,6},{9,14},{10... | collective-permute-start | bytes 786440 | tf_op jit(solution)/shard_map/ppermute | solution.py:262
  148.5 15.2 %collective-permute-start.28 = (f32[64,1024]{1,0:T(8,128)S(1)}, f32[64,1024]{1,0:T(8,128)S(1)}, u32[]{:S(2)}, u32[]{:S(2)}) collective-permute-start(f32[64,1024]{1,0:T(8,128)S(1)} %bitcast_subtract_fusion), channel_id=1, source_target_pairs={{0,8},{1,0},{2,12},{3,4},{4,9},{5,1},{6,13},{7,5},{8,10},{9,2},{10... | collective-permute-start | bytes 786440 | tf_op jit(solution)/shard_map/ppermute | solution.py:262
  157.1 9.5 %collective-permute-start.29 = (f32[64,1024]{1,0:T(8,128)S(1)}, f32[64,1024]{1,0:T(8,128)S(1)}, u32[]{:S(2)}, u32[]{:S(2)}) collective-permute-start(f32[64,1024]{1,0:T(8,128)S(1)} %bitcast_subtract_fusion), channel_id=1, source_target_pairs={{0,12},{1,4},{2,8},{3,0},{4,13},{5,5},{6,9},{7,1},{8,14},{9,6},{10... | collective-permute-start | bytes 786440 | tf_op jit(solution)/shard_map/ppermute | solution.py:262
  159.1 7.5 %copy-start.4 = (f32[64,1024]{1,0:T(8,128)}, f32[64,1024]{1,0:T(8,128)S(1)}, u32[]{:S(2)}) copy-start(f32[64,1024]{1,0:T(8,128)S(1)} %collective-permute-done.26.refs_0_) | copy-start | bytes 786436
  159.1 7.5 %copy-start.5 = (f32[64,1024]{1,0:T(8,128)}, f32[64,1024]{1,0:T(8,128)S(1)}, u32[]{:S(2)}) copy-start(f32[64,1024]{1,0:T(8,128)S(1)} %collective-permute-done.27.refs_1_) | copy-start | bytes 786436
  174.6 7.4 %copy-start.10 = (f32[128,1024]{1,0:T(8,128)S(1)}, f32[128,1024]{1,0:T(8,128)}, u32[]{:S(2)}) copy-start(f32[128,1024]{1,0:T(8,128)} %get-tuple-element.93) | copy-start | bytes 1572868
  174.6 7.4 %collective-permute-start.30 = (f32[128,1024]{1,0:T(8,128)}, f32[128,1024]{1,0:T(8,128)S(1)}, u32[]{:S(2)}, u32[]{:S(2)}) collective-permute-start(f32[128,1024]{1,0:T(8,128)} %get-tuple-element.94), channel_id=1, source_target_pairs={{0,1},{1,0},{2,3},{3,2},{4,5},{5,4},{6,7},{7,6},{8,9},{9,8},{10,11... | collective-permute-start | bytes 1572872 | tf_op jit(solution)/shard_map/ppermute | solution.py:44
  189.4 17.7 %copy-start.8 = (f32[64,1024]{1,0:T(8,128)S(1)}, f32[64,1024]{1,0:T(8,128)}, u32[]{:S(2)}) copy-start(f32[64,1024]{1,0:T(8,128)} %bin_traces.10) | copy-start | bytes 786436
  189.4 17.7 %copy-start.9 = (f32[64,1024]{1,0:T(8,128)S(1)}, f32[64,1024]{1,0:T(8,128)}, u32[]{:S(2)}) copy-start(f32[64,1024]{1,0:T(8,128)} %bin_traces.11) | copy-start | bytes 786436
  189.4 5.4 %collective-permute-start.32 = (f32[128,1024]{1,0:T(8,128)}, f32[128,1024]{1,0:T(8,128)S(1)}, u32[]{:S(2)}, u32[]{:S(2)}) collective-permute-start(f32[128,1024]{1,0:T(8,128)} %get-tuple-element.100), channel_id=1, source_target_pairs={{0,1},{1,0},{2,3},{3,2},{4,5},{5,4},{6,7},{7,6},{8,9},{9,8},{10,11... | collective-permute-start | bytes 1572872 | tf_op jit(solution)/shard_map/ppermute | solution.py:44
  190.0 12.0 %collective-permute-start.31 = (f32[64,1024]{1,0:T(8,128)S(1)}, f32[64,1024]{1,0:T(8,128)S(1)}, u32[]{:S(2)}, u32[]{:S(2)}) collective-permute-start(f32[64,1024]{1,0:T(8,128)S(1)} %slice.127), channel_id=1, source_target_pairs={{0,2},{1,3},{2,0},{3,1},{4,6},{5,7},{6,4},{7,5},{8,10},{9,11},{10,... | collective-permute-start | bytes 786440 | tf_op jit(solution)/shard_map/ppermute | solution.py:44
  196.0 11.0 %collective-permute-start.33 = (f32[64,1024]{1,0:T(8,128)S(1)}, f32[64,1024]{1,0:T(8,128)S(1)}, u32[]{:S(2)}, u32[]{:S(2)}) collective-permute-start(f32[64,1024]{1,0:T(8,128)S(1)} %slice.131), channel_id=1, source_target_pairs={{0,2},{1,3},{2,0},{3,1},{4,6},{5,7},{6,4},{7,5},{8,10},{9,11},{10,... | collective-permute-start | bytes 786440 | tf_op jit(solution)/shard_map/ppermute | solution.py:44
  (13 other events, 26.0 us)

commit v3 on v2

--- a/solution.py
+++ b/solution.py
@@ -278,7 +278,7 @@
     per_tile = LANES // stencil
     units = groups // per_tile
 
-    parts = 2 if fold == 1 else 1
+    parts = 1
     quarters = parts
     part_bins = out_bins // parts
 

time: 209 us -> 201 us (0.962)
  waiting for transfers between devices: 28.1 us -> 50.9 us
  Pallas kernels: 104 us -> 86.4 us
  starting transfers between devices: 59.3 us -> 47.9 us
  other arithmetic: 8.26 us -> 5.5 us
    ppermute x8 -> x4, starting transfers between devices: 30.8 us -> 12.5 us  [spread(): return lax.ppermute(block, ('rcv', 'src'), pairs)]
    ppermute x8 -> x4, waiting for transfers between devices: 11.7 us -> 28.1 us  [spread(): return lax.ppermute(block, ('rcv', 'src'), pairs)]
    pallas_call x6 -> x2, Pallas kernels: 52.9 us -> 37.9 us  [multiply(): pl.pallas_call(functools.partial(multiply_kernel, len(pieces), n_src, len...]
    ppermute x20 -> x16, starting transfers between devices: 18.5 us -> 25.4 us  [swap(): return lax.ppermute(value, axis, [(i, i ^ flip) for i in range(size)])]
    ppermute x20 -> x16, waiting for transfers between devices: 13.2 us -> 19.5 us  [swap(): return lax.ppermute(value, axis, [(i, i ^ flip) for i in range(size)])]
    pallas_call x6 -> x5, Pallas kernels: 50.9 us -> 48.4 us  [bin_step(): pl.pallas_call(functools.partial(bin_kernel, n_block, n_piece, rows, tile...]
    unnamed x55 -> x41, local copies, waits for them, and re-layouts: 4.99 us -> 5.84 us
  transfers between devices with their start and end apart: 34 -> 26, of which waited for: 12 -> 11; matrix products, arithmetic and copies ran while one was open for 3% -> 2% of each run, Pallas kernels for 27% -> 19%
where the time goes in v3:
time: 201 us; the launch traced here: 200 us
  Pallas kernels  86.4 us (43%)
  waiting for transfers between devices  50.9 us (25%)
  starting transfers between devices  47.9 us (24%)
  local copies, waits for them, and re-layouts  9.3 us (5%)
  other arithmetic  5.5 us (3%)
    pallas_call x5, Pallas kernels, bin_step(): pl.pallas_call(functools.partial(bin_kernel, n_block, n_piece, rows, tile...  48.4 us
    pallas_call x2, Pallas kernels, multiply(): pl.pallas_call(functools.partial(multiply_kernel, len(pieces), n_src, len...  37.9 us
    ppermute x4, waiting for transfers between devices, spread(): return lax.ppermute(block, ('rcv', 'src'), pairs)  28.1 us
    ppermute x16, starting transfers between devices, swap(): return lax.ppermute(value, axis, [(i, i ^ flip) for i in range(size)])  25.4 us
    ppermute x16, waiting for transfers between devices, swap(): return lax.ppermute(value, axis, [(i, i ^ flip) for i in range(size)])  19.5 us
    ppermute x4, starting transfers between devices, spread(): return lax.ppermute(block, ('rcv', 'src'), pairs)  12.5 us
    ppermute x3, starting transfers between devices, line_step(): by_shift[-step] = lax.ppermute(below, 'rcv', up)  6.1 us
    unnamed x41, local copies, waits for them, and re-layouts  5.84 us
  transfers between devices with their start and end apart: 26, of which 11 were waited for; matrix products, arithmetic and copies ran while one was open for 2% of the time, Pallas kernels for 19%

profile of v3, /device:TPU:0, one launch (start us, length us, event | category | flops | bytes accessed | tf_op | source)
XLA Modules:
  0.0 200.3 jit_solution(10657732834953157356)
XLA Ops:
  0.0 1.0 copy.12
  1.0 0.7 add_convert_fusion
  1.8 3.0 %collective-permute-start = (f32[72,1024]{1,0:T(8,128)S(1)}, f32[72,1024]{1,0:T(8,128)S(1)}, u32[]{:S(2)}, u32[]{:S(2)}) collective-permute-start(f32[72,1024]{1,0:T(8,128)S(1)} %pad_maximum_fusion.1.refs_0_), channel_id=1, source_target_pairs={{0,2},{1,3},{2,0},{3,1},{4,6},{5,7},{6,4},{7,5},{8,10},{9,11},{10,... | collective-permute-start | bytes 884744 | tf_op jit(solution)/shard_map/ppermute | solution.py:44
  4.8 1.3 collective-permute-start.3
  6.1 4.6 %collective-permute-start.4 = (f32[72,1024]{1,0:T(8,128)S(1)}, f32[72,1024]{1,0:T(8,128)S(1)}, u32[]{:S(2)}, u32[]{:S(2)}) collective-permute-start(f32[72,1024]{1,0:T(8,128)S(1)} %pad_maximum_fusion.1.refs_0_), channel_id=1, source_target_pairs={{0,4},{4,8},{8,12},{1,5},{5,9},{9,13},{2,6},{6,10},{10,14},{3,7},{... | collective-permute-start | bytes 884744 | tf_op jit(solution)/shard_map/ppermute | solution.py:52
  10.7 1.1 collective-permute-done.refs_2_
  11.8 0.5 collective-permute-start.2
  12.3 0.9 multiply_bitcast_fusion
  13.5 0.8 copy.16.matrix_ref
  14.4 0.8 collective-permute-done.3
  15.2 1.2 collective-permute-done.4
  16.4 1.3 collective-permute-start.8
  17.7 0.7 collective-permute-start.9
  18.9 0.7 copy-done.14
  19.5 7.7 %bin_traces.5.refs_0_ = f32[256,4096]{1,0:T(8,128)} custom-call(s32[1]{0:T(128)} %bitcast.2.origin_ref, f32[256,256]{1,0:T(8,128)} %copy.16.matrix_ref, f32[72,1024]{1,0:T(8,128)} %copy-done.4, f32[72,1024]{1,0:T(8,128)} %copy-done.14, f32[72,1024]{1,0:T(8,128)} %copy-done.13, f32[72,1024]{1,0:T(8,128)} %collective-permute-done.2.refs_3_), custom_call_target="tpu_custom_call" | custom-call | flops 4294967296 | bytes 4194304 | tf_op jit(solution)/shard_map/bin_traces/pallas_call | solution.py:167
  27.3 0.5 collective-permute-start.7
  27.9 1.3 collective-permute-start.13
  29.2 0.9 collective-permute-start.14
  30.0 1.7 collective-permute-start.10
  31.8 0.7 copy-done.18
  32.5 8.4 %bin_traces.6.refs_0_ = f32[256,4096]{1,0:T(8,128)} custom-call(s32[1]{0:T(128)} %bitcast.2.origin_ref, f32[256,256]{1,0:T(8,128)} %copy.16.matrix_ref, f32[256,4096]{1,0:T(8,128)} %bin_traces.5.refs_0_, f32[72,1024]{1,0:T(8,128)} %copy-done.2, f32[72,1024]{1,0:T(8,128)} %copy-done.18, f32[72,1024]{1,0:T(8,128)} %copy-done.16, ...), custom_call_target="tpu_custom_call" | custom-call | flops 4294967296 | bytes 4194304 | tf_op jit(solution)/shard_map/bin_traces/pallas_call | solution.py:167
  41.4 1.3 collective-permute-done.13
  42.9 1.7 collective-permute-start.15
  44.6 0.7 copy-done.17
  45.3 0.7 copy-done.19
  46.0 8.4 %bin_traces.7.refs_0_ = f32[256,4096]{1,0:T(8,128)} custom-call(s32[1]{0:T(128)} %bitcast.2.origin_ref, f32[256,256]{1,0:T(8,128)} %copy.16.matrix_ref, f32[256,4096]{1,0:T(8,128)} %bin_traces.6.refs_0_, f32[72,1024]{1,0:T(8,128)} %copy-done.3, f32[72,1024]{1,0:T(8,128)} %copy-done.17, f32[72,1024]{1,0:T(8,128)} %copy-done.15, f32[72,1024]{1,0:T(8,128)} %copy-done.19), custom_call_target="tpu_custom_call" | custom-call | flops 4294967296 | bytes 4194304 | tf_op jit(solution)/shard_map/bin_traces/pallas_call | solution.py:167
  55.0 0.6 pad_add_fusion.order_ref
  56.8 0.7 copy-done.12
  57.5 9.6 %bin_traces.8.refs_0_ = bf16[2,256,2048]{2,1,0:T(8,128)(2,1)} custom-call(s32[1]{0:T(128)} %bitcast.2.origin_ref, f32[256,256]{1,0:T(8,128)} %copy.16.matrix_ref, f32[256,4096]{1,0:T(8,128)} %bin_traces.7.refs_0_, f32[72,1024]{1,0:T(8,128)} %copy-done.5, f32[72,1024]{1,0:T(8,128)} %copy-done.11, f32[72,1024]{1,0:T(8,128)} %copy-done.10, f32[72,1024]{1,0:T(8,128)} %copy-done.12), custom_call_target="tpu_custom_call" | custom-call | flops 4294967296 | bytes 4194304 | tf_op jit(solution)/shard_map/bin_traces/pallas_call | solution.py:167
  67.1 18.8 %multiply.3 = (f32[128,2048]{1,0:T(8,128)}, f32[128,2048]{1,0:T(8,128)}) custom-call(s32[2]{0:T(128)} %pad_add_fusion.order_ref, f32[2,2048,2048]{2,1,0:T(8,128)} %a_ref.3, bf16[2,256,2048]{2,1,0:T(8,128)(2,1)} %bin_traces.8.refs_0_), custom_call_target="tpu_custom_call" | custom-call | flops 12884901888 | bytes 33554432 | tf_op jit(solution)/shard_map/multiply/pallas_call | solution.py:233
  86.0 2.7 %collective-permute-done.18 = f32[128,2048]{1,0:T(8,128)S(1)} collective-permute-done((f32[128,2048]{1,0:T(8,128)}, f32[128,2048]{1,0:T(8,128)S(1)}, u32[]{:S(2)}, u32[]{:S(2)}) %collective-permute-start.18) | collective-permute-done | bytes 1048608 | tf_op jit(solution)/shard_map/ppermute | solution.py:44
  88.7 1.3 add.40
  90.8 14.5 %bin_traces.9 = f32[64,2048]{1,0:T(8,128)} custom-call(s32[1]{0:T(128)} %bitcast.6.origin_ref, f32[256,256]{1,0:T(8,128)} %copy.16.matrix_ref, f32[72,1024]{1,0:T(8,128)} %copy-done.4, f32[72,1024]{1,0:T(8,128)} %copy-done.2, f32[72,1024]{1,0:T(8,128)} %copy-done.3, f32[72,1024]{1,0:T(8,128)} %copy-done.5), custom_call_target="tpu_custom_call" | custom-call | flops 4294967296 | bytes 1048576 | tf_op jit(solution)/shard_map/bin_traces/pallas_call | solution.py:167
  105.5 0.9 copy-done
  106.4 0.7 collective-permute-start.20
  107.1 6.3 %collective-permute-start.21 = (f32[64,2048]{1,0:T(8,128)S(1)}, f32[64,2048]{1,0:T(8,128)S(1)}, u32[]{:S(2)}, u32[]{:S(2)}) collective-permute-start(f32[64,2048]{1,0:T(8,128)S(1)} %bitcast_subtract_fusion), channel_id=1, source_target_pairs={{0,4},{1,12},{2,0},{3,8},{4,5},{5,13},{6,1},{7,9},{8,6},{9,14},{10... | collective-permute-start | bytes 1572872 | tf_op jit(solution)/shard_map/ppermute | solution.py:262
  113.5 2.4 %collective-permute-start.22 = (f32[64,2048]{1,0:T(8,128)S(1)}, f32[64,2048]{1,0:T(8,128)S(1)}, u32[]{:S(2)}, u32[]{:S(2)}) collective-permute-start(f32[64,2048]{1,0:T(8,128)S(1)} %bitcast_subtract_fusion), channel_id=1, source_target_pairs={{0,8},{1,0},{2,12},{3,4},{4,9},{5,1},{6,13},{7,5},{8,10},{9,2},{10... | collective-permute-start | bytes 1572872 | tf_op jit(solution)/shard_map/ppermute | solution.py:262
  115.8 3.1 %collective-permute-start.23 = (f32[64,2048]{1,0:T(8,128)S(1)}, f32[64,2048]{1,0:T(8,128)S(1)}, u32[]{:S(2)}, u32[]{:S(2)}) collective-permute-start(f32[64,2048]{1,0:T(8,128)S(1)} %bitcast_subtract_fusion), channel_id=1, source_target_pairs={{0,12},{1,4},{2,8},{3,0},{4,13},{5,5},{6,9},{7,1},{8,14},{9,6},{10... | collective-permute-start | bytes 1572872 | tf_op jit(solution)/shard_map/ppermute | solution.py:262
  119.0 19.2 %collective-permute-done.21.refs_1_ = f32[64,2048]{1,0:T(8,128)S(1)} collective-permute-done((f32[64,2048]{1,0:T(8,128)S(1)}, f32[64,2048]{1,0:T(8,128)S(1)}, u32[]{:S(2)}, u32[]{:S(2)}) %collective-permute-start.21) | collective-permute-done | bytes 524320 | tf_op jit(solution)/shard_map/ppermute | solution.py:262
  138.2 8.9 %collective-permute-done.23.refs_3_ = f32[64,2048]{1,0:T(8,128)S(1)} collective-permute-done((f32[64,2048]{1,0:T(8,128)S(1)}, f32[64,2048]{1,0:T(8,128)S(1)}, u32[]{:S(2)}, u32[]{:S(2)}) %collective-permute-start.23) | collective-permute-done | bytes 524320 | tf_op jit(solution)/shard_map/ppermute | solution.py:262
  147.1 0.8 copy-done.9
  147.9 19.2 %multiply.4 = (f32[128,2048]{1,0:T(8,128)}, f32[128,2048]{1,0:T(8,128)}) custom-call(s32[2]{0:T(128)} %pad_add_fusion.order_ref, f32[2,2048,2048]{2,1,0:T(8,128)} %a_ref.3, f32[64,2048]{1,0:T(8,128)} %copy-done.6, f32[64,2048]{1,0:T(8,128)} %copy-done.7, f32[64,2048]{1,0:T(8,128)} %copy-done.8, f32[64,2048]{1,0:T(8,128)} %copy-done.9), custom_call_target="tpu_custom_call" | custom-call | flops 12884901888 | bytes 33554432 | tf_op jit(solution)/shard_map/multiply/pallas_call | solution.py:233
  167.0 0.8 collective-permute-start.24
  167.9 2.5 %collective-permute-done.24 = f32[128,2048]{1,0:T(8,128)S(1)} collective-permute-done((f32[128,2048]{1,0:T(8,128)}, f32[128,2048]{1,0:T(8,128)S(1)}, u32[]{:S(2)}, u32[]{:S(2)}) %collective-permute-start.24) | collective-permute-done | bytes 1048608 | tf_op jit(solution)/shard_map/ppermute | solution.py:44
  170.4 1.3 add.43
  171.8 14.9 %collective-permute-start.25 = (f32[64,2048]{1,0:T(8,128)S(1)}, f32[64,2048]{1,0:T(8,128)S(1)}, u32[]{:S(2)}, u32[]{:S(2)}) collective-permute-start(f32[64,2048]{1,0:T(8,128)S(1)} %slice.61), channel_id=1, source_target_pairs={{0,2},{1,3},{2,0},{3,1},{4,6},{5,7},{6,4},{7,5},{8,10},{9,11},{10,... | collective-permute-start | bytes 1572872 | tf_op jit(solution)/shard_map/ppermute | solution.py:44
  186.6 12.2 %collective-permute-done.25 = f32[64,2048]{1,0:T(8,128)S(1)} collective-permute-done((f32[64,2048]{1,0:T(8,128)S(1)}, f32[64,2048]{1,0:T(8,128)S(1)}, u32[]{:S(2)}, u32[]{:S(2)}) %collective-permute-start.25) | collective-permute-done | bytes 524320 | tf_op jit(solution)/shard_map/ppermute | solution.py:44
  199.1 1.2 copy.19
  (76 shorter events, 4.8 us)
Async XLA Ops:
  1.8 17.0 %copy-start.4 = (f32[72,1024]{1,0:T(8,128)}, f32[72,1024]{1,0:T(8,128)S(1)}, u32[]{:S(2)}) copy-start(f32[72,1024]{1,0:T(8,128)S(1)} %pad_maximum_fusion.1.refs_0_) | copy-start | bytes 884740
  1.8 10.0 %collective-permute-start = (f32[72,1024]{1,0:T(8,128)S(1)}, f32[72,1024]{1,0:T(8,128)S(1)}, u32[]{:S(2)}, u32[]{:S(2)}) collective-permute-start(f32[72,1024]{1,0:T(8,128)S(1)} %pad_maximum_fusion.1.refs_0_), channel_id=1, source_target_pairs={{0,2},{1,3},{2,0},{3,1},{4,6},{5,7},{6,4},{7,5},{8,10},{9,11},{10,... | collective-permute-start | bytes 884744 | tf_op jit(solution)/shard_map/ppermute | solution.py:44
  4.8 10.3 %collective-permute-start.3 = (f32[72,1024]{1,0:T(8,128)S(1)}, f32[72,1024]{1,0:T(8,128)S(1)}, u32[]{:S(2)}, u32[]{:S(2)}) collective-permute-start(f32[72,1024]{1,0:T(8,128)S(1)} %pad_maximum_fusion.1.refs_0_), channel_id=1, source_target_pairs={{4,0},{8,4},{12,8},{5,1},{9,5},{13,9},{6,2},{10,6},{14,10},{7,3},{... | collective-permute-start | bytes 884744 | tf_op jit(solution)/shard_map/ppermute | solution.py:53
  6.1 10.2 %collective-permute-start.4 = (f32[72,1024]{1,0:T(8,128)S(1)}, f32[72,1024]{1,0:T(8,128)S(1)}, u32[]{:S(2)}, u32[]{:S(2)}) collective-permute-start(f32[72,1024]{1,0:T(8,128)S(1)} %pad_maximum_fusion.1.refs_0_), channel_id=1, source_target_pairs={{0,4},{4,8},{8,12},{1,5},{5,9},{9,13},{2,6},{6,10},{10,14},{3,7},{... | collective-permute-start | bytes 884744 | tf_op jit(solution)/shard_map/ppermute | solution.py:52
  11.8 7.0 %copy-start.13 = (f32[72,1024]{1,0:T(8,128)}, f32[72,1024]{1,0:T(8,128)S(1)}, u32[]{:S(2)}) copy-start(f32[72,1024]{1,0:T(8,128)S(1)} %collective-permute-done.refs_2_) | copy-start | bytes 884740
  11.8 7.0 %collective-permute-start.1 = (f32[72,1024]{1,0:T(8,128)S(1)}, f32[72,1024]{1,0:T(8,128)S(1)}, u32[]{:S(2)}, u32[]{:S(2)}) collective-permute-start(f32[72,1024]{1,0:T(8,128)S(1)} %pad_maximum_fusion.1.refs_0_), channel_id=1, source_target_pairs={{0,1},{1,0},{2,3},{3,2},{4,5},{5,4},{6,7},{7,6},{8,9},{9,8},{10,11... | collective-permute-start | bytes 884744 | tf_op jit(solution)/shard_map/ppermute | solution.py:44
  11.8 7.0 %collective-permute-start.2 = (f32[72,1024]{1,0:T(8,128)S(1)}, f32[72,1024]{1,0:T(8,128)}, u32[]{:S(2)}, u32[]{:S(2)}) collective-permute-start(f32[72,1024]{1,0:T(8,128)S(1)} %collective-permute-done.refs_2_), channel_id=1, source_target_pairs={{0,1},{1,0},{2,3},{3,2},{4,5},{5,4},{6,7},{7,6},{8,9},{9,8},{10,11... | collective-permute-start | bytes 884744 | tf_op jit(solution)/shard_map/ppermute | solution.py:44
  16.4 10.8 %copy-start.2 = (f32[72,1024]{1,0:T(8,128)}, f32[72,1024]{1,0:T(8,128)S(1)}, u32[]{:S(2)}) copy-start(f32[72,1024]{1,0:T(8,128)S(1)} %broadcast_select_fusion.1.refs_1_) | copy-start | bytes 884740
  16.4 11.4 %collective-permute-start.8 = (f32[72,1024]{1,0:T(8,128)S(1)}, f32[72,1024]{1,0:T(8,128)S(1)}, u32[]{:S(2)}, u32[]{:S(2)}) collective-permute-start(f32[72,1024]{1,0:T(8,128)S(1)} %collective-permute-done.3), channel_id=1, source_target_pairs={{4,0},{8,4},{5,1},{9,5},{6,2},{10,6},{7,3},{11,7},{20,16},{24,20},... | collective-permute-start | bytes 884744 | tf_op jit(solution)/shard_map/ppermute | solution.py:53
  17.7 10.1 %collective-permute-start.9 = (f32[72,1024]{1,0:T(8,128)S(1)}, f32[72,1024]{1,0:T(8,128)S(1)}, u32[]{:S(2)}, u32[]{:S(2)}) collective-permute-start(f32[72,1024]{1,0:T(8,128)S(1)} %collective-permute-done.4), channel_id=1, source_target_pairs={{4,8},{8,12},{5,9},{9,13},{6,10},{10,14},{7,11},{11,15},{20,24},{2... | collective-permute-start | bytes 884744 | tf_op jit(solution)/shard_map/ppermute | solution.py:52
  18.4 8.8 %collective-permute-start.5 = (f32[72,1024]{1,0:T(8,128)S(1)}, f32[72,1024]{1,0:T(8,128)S(1)}, u32[]{:S(2)}, u32[]{:S(2)}) collective-permute-start(f32[72,1024]{1,0:T(8,128)S(1)} %broadcast_select_fusion.1.refs_1_), channel_id=1, source_target_pairs={{0,2},{1,3},{2,0},{3,1},{4,6},{5,7},{6,4},{7,5},{8,10},{9,11},{10,... | collective-permute-start | bytes 884744 | tf_op jit(solution)/shard_map/ppermute | solution.py:44
  18.8 0.7 copy-start.14
  27.2 4.5 %copy-start.16 = (f32[72,1024]{1,0:T(8,128)}, f32[72,1024]{1,0:T(8,128)S(1)}, u32[]{:S(2)}) copy-start(f32[72,1024]{1,0:T(8,128)S(1)} %collective-permute-done.5.refs_3_) | copy-start | bytes 884740
  27.2 4.5 %collective-permute-start.6 = (f32[72,1024]{1,0:T(8,128)S(1)}, f32[72,1024]{1,0:T(8,128)S(1)}, u32[]{:S(2)}, u32[]{:S(2)}) collective-permute-start(f32[72,1024]{1,0:T(8,128)S(1)} %broadcast_select_fusion.1.refs_1_), channel_id=1, source_target_pairs={{0,1},{1,0},{2,3},{3,2},{4,5},{5,4},{6,7},{7,6},{8,9},{9,8},{10,11... | collective-permute-start | bytes 884744 | tf_op jit(solution)/shard_map/ppermute | solution.py:44
  27.3 4.5 %collective-permute-start.7 = (f32[72,1024]{1,0:T(8,128)S(1)}, f32[72,1024]{1,0:T(8,128)}, u32[]{:S(2)}, u32[]{:S(2)}) collective-permute-start(f32[72,1024]{1,0:T(8,128)S(1)} %collective-permute-done.5.refs_3_), channel_id=1, source_target_pairs={{0,1},{1,0},{2,3},{3,2},{4,5},{5,4},{6,7},{7,6},{8,9},{9,8},{10,11... | collective-permute-start | bytes 884744 | tf_op jit(solution)/shard_map/ppermute | solution.py:44
  27.8 13.0 %copy-start.3 = (f32[72,1024]{1,0:T(8,128)}, f32[72,1024]{1,0:T(8,128)S(1)}, u32[]{:S(2)}) copy-start(f32[72,1024]{1,0:T(8,128)S(1)} %broadcast_select_fusion.refs_1_.refs_2_) | copy-start | bytes 884740
  27.9 14.9 %collective-permute-start.13 = (f32[72,1024]{1,0:T(8,128)S(1)}, f32[72,1024]{1,0:T(8,128)S(1)}, u32[]{:S(2)}, u32[]{:S(2)}) collective-permute-start(f32[72,1024]{1,0:T(8,128)S(1)} %collective-permute-done.8), channel_id=1, source_target_pairs={{4,0},{5,1},{6,2},{7,3},{20,16},{21,17},{22,18},{23,19}} | collective-permute-start | bytes 884744 | tf_op jit(solution)/shard_map/ppermute | solution.py:53
  29.2 13.6 %collective-permute-start.14 = (f32[72,1024]{1,0:T(8,128)S(1)}, f32[72,1024]{1,0:T(8,128)S(1)}, u32[]{:S(2)}, u32[]{:S(2)}) collective-permute-start(f32[72,1024]{1,0:T(8,128)S(1)} %collective-permute-done.9), channel_id=1, source_target_pairs={{8,12},{9,13},{10,14},{11,15},{24,28},{25,29},{26,30},{27,31}} | collective-permute-start | bytes 884744 | tf_op jit(solution)/shard_map/ppermute | solution.py:52
  30.0 10.8 %collective-permute-start.10 = (f32[72,1024]{1,0:T(8,128)S(1)}, f32[72,1024]{1,0:T(8,128)S(1)}, u32[]{:S(2)}, u32[]{:S(2)}) collective-permute-start(f32[72,1024]{1,0:T(8,128)S(1)} %broadcast_select_fusion.refs_1_.refs_2_), channel_id=1, source_target_pairs={{0,2},{1,3},{2,0},{3,1},{4,6},{5,7},{6,4},{7,5},{8,10},{9,11},{10,... | collective-permute-start | bytes 884744 | tf_op jit(solution)/shard_map/ppermute | solution.py:44
  31.8 0.7 copy-start.18
  40.8 3.7 %copy-start.15 = (f32[72,1024]{1,0:T(8,128)}, f32[72,1024]{1,0:T(8,128)S(1)}, u32[]{:S(2)}) copy-start(f32[72,1024]{1,0:T(8,128)S(1)} %collective-permute-done.10.refs_3_) | copy-start | bytes 884740
  40.9 3.7 %collective-permute-start.11 = (f32[72,1024]{1,0:T(8,128)S(1)}, f32[72,1024]{1,0:T(8,128)S(1)}, u32[]{:S(2)}, u32[]{:S(2)}) collective-permute-start(f32[72,1024]{1,0:T(8,128)S(1)} %broadcast_select_fusion.refs_1_.refs_2_), channel_id=1, source_target_pairs={{0,1},{1,0},{2,3},{3,2},{4,5},{5,4},{6,7},{7,6},{8,9},{9,8},{10,11... | collective-permute-start | bytes 884744 | tf_op jit(solution)/shard_map/ppermute | solution.py:44
  40.9 3.6 %collective-permute-start.12 = (f32[72,1024]{1,0:T(8,128)S(1)}, f32[72,1024]{1,0:T(8,128)S(1)}, u32[]{:S(2)}, u32[]{:S(2)}) collective-permute-start(f32[72,1024]{1,0:T(8,128)S(1)} %collective-permute-done.10.refs_3_), channel_id=1, source_target_pairs={{0,1},{1,0},{2,3},{3,2},{4,5},{5,4},{6,7},{7,6},{8,9},{9,8},{10,11... | collective-permute-start | bytes 884744 | tf_op jit(solution)/shard_map/ppermute | solution.py:44
  42.8 11.5 %copy-start.5 = (f32[72,1024]{1,0:T(8,128)}, f32[72,1024]{1,0:T(8,128)S(1)}, u32[]{:S(2)}) copy-start(f32[72,1024]{1,0:T(8,128)S(1)} %select_select_fusion.refs_1_.refs_3_) | copy-start | bytes 884740
  42.9 11.5 %collective-permute-start.15 = (f32[72,1024]{1,0:T(8,128)S(1)}, f32[72,1024]{1,0:T(8,128)S(1)}, u32[]{:S(2)}, u32[]{:S(2)}) collective-permute-start(f32[72,1024]{1,0:T(8,128)S(1)} %select_select_fusion.refs_1_.refs_3_), channel_id=1, source_target_pairs={{0,2},{1,3},{2,0},{3,1},{4,6},{5,7},{6,4},{7,5},{8,10},{9,11},{10,... | collective-permute-start | bytes 884744 | tf_op jit(solution)/shard_map/ppermute | solution.py:44
  44.6 0.7 copy-start.17
  45.3 0.7 copy-start.19
  54.4 2.1 %copy-start.10 = (f32[72,1024]{1,0:T(8,128)}, f32[72,1024]{1,0:T(8,128)S(1)}, u32[]{:S(2)}) copy-start(f32[72,1024]{1,0:T(8,128)S(1)} %collective-permute-done.15.refs_3_) | copy-start | bytes 884740
  54.4 1.6 collective-permute-start.16
  54.5 2.0 collective-permute-start.17
  56.1 0.7 copy-start.11
  56.8 0.7 copy-start.12
  85.8 4.7 %copy-start.1 = (f32[32,2,2048]{2,1,0:T(2,128)S(1)}, f32[32,2,2048]{2,1,0:T(2,128)}, u32[]{:S(2)}) copy-start(f32[32,2,2048]{2,1,0:T(2,128)} %param.13) | copy-start | bytes 1572868
  85.8 2.9 %collective-permute-start.18 = (f32[128,2048]{1,0:T(8,128)}, f32[128,2048]{1,0:T(8,128)S(1)}, u32[]{:S(2)}, u32[]{:S(2)}) collective-permute-start(f32[128,2048]{1,0:T(8,128)} %get-tuple-element.67), channel_id=1, source_target_pairs={{0,1},{1,0},{2,3},{3,2},{4,5},{5,4},{6,7},{7,6},{8,9},{9,8},{10,11... | collective-permute-start | bytes 3145736 | tf_op jit(solution)/shard_map/ppermute | solution.py:44
  90.1 15.2 %collective-permute-start.19 = (f32[64,2048]{1,0:T(8,128)S(1)}, f32[64,2048]{1,0:T(8,128)S(1)}, u32[]{:S(2)}, u32[]{:S(2)}) collective-permute-start(f32[64,2048]{1,0:T(8,128)S(1)} %slice.56), channel_id=1, source_target_pairs={{0,2},{1,3},{2,0},{3,1},{4,6},{5,7},{6,4},{7,5},{8,10},{9,11},{10,... | collective-permute-start | bytes 1572872 | tf_op jit(solution)/shard_map/ppermute | solution.py:44
  105.3 1.0 copy-start
  106.4 12.6 %collective-permute-start.20 = (f32[64,2048]{1,0:T(8,128)S(1)}, f32[64,2048]{1,0:T(8,128)S(1)}, u32[]{:S(2)}, u32[]{:S(2)}) collective-permute-start(f32[64,2048]{1,0:T(8,128)S(1)} %bitcast_subtract_fusion), channel_id=1, source_target_pairs={{0,0},{1,8},{2,4},{3,12},{4,1},{5,9},{6,5},{7,13},{8,2},{9,10},{10... | collective-permute-start | bytes 1572872 | tf_op jit(solution)/shard_map/ppermute | solution.py:262
  107.1 31.0 %collective-permute-start.21 = (f32[64,2048]{1,0:T(8,128)S(1)}, f32[64,2048]{1,0:T(8,128)S(1)}, u32[]{:S(2)}, u32[]{:S(2)}) collective-permute-start(f32[64,2048]{1,0:T(8,128)S(1)} %bitcast_subtract_fusion), channel_id=1, source_target_pairs={{0,4},{1,12},{2,0},{3,8},{4,5},{5,13},{6,1},{7,9},{8,6},{9,14},{10... | collective-permute-start | bytes 1572872 | tf_op jit(solution)/shard_map/ppermute | solution.py:262
  113.5 24.7 %collective-permute-start.22 = (f32[64,2048]{1,0:T(8,128)S(1)}, f32[64,2048]{1,0:T(8,128)S(1)}, u32[]{:S(2)}, u32[]{:S(2)}) collective-permute-start(f32[64,2048]{1,0:T(8,128)S(1)} %bitcast_subtract_fusion), channel_id=1, source_target_pairs={{0,8},{1,0},{2,12},{3,4},{4,9},{5,1},{6,13},{7,5},{8,10},{9,2},{10... | collective-permute-start | bytes 1572872 | tf_op jit(solution)/shard_map/ppermute | solution.py:262
  115.8 31.2 %collective-permute-start.23 = (f32[64,2048]{1,0:T(8,128)S(1)}, f32[64,2048]{1,0:T(8,128)S(1)}, u32[]{:S(2)}, u32[]{:S(2)}) collective-permute-start(f32[64,2048]{1,0:T(8,128)S(1)} %bitcast_subtract_fusion), channel_id=1, source_target_pairs={{0,12},{1,4},{2,8},{3,0},{4,13},{5,5},{6,9},{7,1},{8,14},{9,6},{10... | collective-permute-start | bytes 1572872 | tf_op jit(solution)/shard_map/ppermute | solution.py:262
  119.0 28.1 %copy-start.6 = (f32[64,2048]{1,0:T(8,128)}, f32[64,2048]{1,0:T(8,128)S(1)}, u32[]{:S(2)}) copy-start(f32[64,2048]{1,0:T(8,128)S(1)} %collective-permute-done.20.refs_0_) | copy-start | bytes 1572868
  138.2 8.9 %copy-start.7 = (f32[64,2048]{1,0:T(8,128)}, f32[64,2048]{1,0:T(8,128)S(1)}, u32[]{:S(2)}) copy-start(f32[64,2048]{1,0:T(8,128)S(1)} %collective-permute-done.21.refs_1_) | copy-start | bytes 1572868
  138.2 8.9 %copy-start.8 = (f32[64,2048]{1,0:T(8,128)}, f32[64,2048]{1,0:T(8,128)S(1)}, u32[]{:S(2)}) copy-start(f32[64,2048]{1,0:T(8,128)S(1)} %collective-permute-done.22.refs_2_) | copy-start | bytes 1572868
  147.1 0.8 copy-start.9
  167.0 3.3 %collective-permute-start.24 = (f32[128,2048]{1,0:T(8,128)}, f32[128,2048]{1,0:T(8,128)S(1)}, u32[]{:S(2)}, u32[]{:S(2)}) collective-permute-start(f32[128,2048]{1,0:T(8,128)} %get-tuple-element.70), channel_id=1, source_target_pairs={{0,1},{1,0},{2,3},{3,2},{4,5},{5,4},{6,7},{7,6},{8,9},{9,8},{10,11... | collective-permute-start | bytes 3145736 | tf_op jit(solution)/shard_map/ppermute | solution.py:44
  171.8 27.1 %collective-permute-start.25 = (f32[64,2048]{1,0:T(8,128)S(1)}, f32[64,2048]{1,0:T(8,128)S(1)}, u32[]{:S(2)}, u32[]{:S(2)}) collective-permute-start(f32[64,2048]{1,0:T(8,128)S(1)} %slice.61), channel_id=1, source_target_pairs={{0,2},{1,3},{2,0},{3,1},{4,6},{5,7},{6,4},{7,5},{8,10},{9,11},{10,... | collective-permute-start | bytes 1572872 | tf_op jit(solution)/shard_map/ppermute | solution.py:44

commit v4 on v3

--- a/solution.py
+++ b/solution.py
@@ -151,7 +151,7 @@
     n_block, n_piece = len(pieces), len(pieces[0])
     length = pieces[0][0].shape[1]
     all_rows = n_piece * rows
-    tile_units = min(4, units)
+    tile_units = min(8, units)
     tiles = units // tile_units
     width = matrix.shape[0] * tile_units
     lanes = LANES * tile_units

time: 201 us -> 201 us (level)
  no operation moved by 1% of the time
where the time goes in v4:
time: 201 us; the launch traced here: 200 us
  Pallas kernels  85.9 us (43%)
  waiting for transfers between devices  51.2 us (25%)
  starting transfers between devices  47.5 us (24%)
  local copies, waits for them, and re-layouts  9.3 us (5%)
  other arithmetic  5.5 us (3%)
    pallas_call x5, Pallas kernels, bin_step(): pl.pallas_call(functools.partial(bin_kernel, n_block, n_piece, rows, tile...  47.9 us
    pallas_call x2, Pallas kernels, multiply(): pl.pallas_call(functools.partial(multiply_kernel, len(pieces), n_src, len...  37.9 us
    ppermute x4, waiting for transfers between devices, spread(): return lax.ppermute(block, ('rcv', 'src'), pairs)  28.3 us
    ppermute x16, starting transfers between devices, swap(): return lax.ppermute(value, axis, [(i, i ^ flip) for i in range(size)])  25.4 us
    ppermute x16, waiting for transfers between devices, swap(): return lax.ppermute(value, axis, [(i, i ^ flip) for i in range(size)])  19.5 us
    ppermute x4, starting transfers between devices, spread(): return lax.ppermute(block, ('rcv', 'src'), pairs)  12.2 us
    ppermute x3, starting transfers between devices, line_step(): by_shift[-step] = lax.ppermute(below, 'rcv', up)  6.1 us
    unnamed x41, local copies, waits for them, and re-layouts  5.84 us
  transfers between devices with their start and end apart: 26, of which 11 were waited for; matrix products, arithmetic and copies ran while one was open for 2% of the time, Pallas kernels for 19%

profile of v4, /device:TPU:0, one launch (start us, length us, event | category | flops | bytes accessed | tf_op | source)
XLA Modules:
  0.0 199.8 jit_solution(4799440924329393124)
XLA Ops:
  0.0 1.0 copy.12
  1.0 0.7 add_convert_fusion
  1.8 3.0 %collective-permute-start = (f32[72,1024]{1,0:T(8,128)S(1)}, f32[72,1024]{1,0:T(8,128)S(1)}, u32[]{:S(2)}, u32[]{:S(2)}) collective-permute-start(f32[72,1024]{1,0:T(8,128)S(1)} %pad_maximum_fusion.1.refs_0_), channel_id=1, source_target_pairs={{0,2},{1,3},{2,0},{3,1},{4,6},{5,7},{6,4},{7,5},{8,10},{9,11},{10,... | collective-permute-start | bytes 884744 | tf_op jit(solution)/shard_map/ppermute | solution.py:44
  4.8 1.3 collective-permute-start.3
  6.1 4.6 %collective-permute-start.4 = (f32[72,1024]{1,0:T(8,128)S(1)}, f32[72,1024]{1,0:T(8,128)S(1)}, u32[]{:S(2)}, u32[]{:S(2)}) collective-permute-start(f32[72,1024]{1,0:T(8,128)S(1)} %pad_maximum_fusion.1.refs_0_), channel_id=1, source_target_pairs={{0,4},{4,8},{8,12},{1,5},{5,9},{9,13},{2,6},{6,10},{10,14},{3,7},{... | collective-permute-start | bytes 884744 | tf_op jit(solution)/shard_map/ppermute | solution.py:52
  10.7 1.1 collective-permute-done.refs_2_
  11.8 0.5 collective-permute-start.2
  12.3 0.9 multiply_bitcast_fusion
  13.5 0.8 copy.16.matrix_ref
  14.4 0.8 collective-permute-done.3
  15.2 1.2 collective-permute-done.4
  16.4 1.3 collective-permute-start.8
  17.7 0.7 collective-permute-start.9
  18.9 0.7 copy-done.14
  19.5 7.6 %bin_traces.5.refs_0_ = f32[256,4096]{1,0:T(8,128)} custom-call(s32[1]{0:T(128)} %bitcast.2.origin_ref, f32[256,256]{1,0:T(8,128)} %copy.16.matrix_ref, f32[72,1024]{1,0:T(8,128)} %copy-done.4, f32[72,1024]{1,0:T(8,128)} %copy-done.14, f32[72,1024]{1,0:T(8,128)} %copy-done.13, f32[72,1024]{1,0:T(8,128)} %collective-permute-done.2.refs_3_), custom_call_target="tpu_custom_call" | custom-call | flops 4294967296 | bytes 4194304 | tf_op jit(solution)/shard_map/bin_traces/pallas_call | solution.py:167
  27.2 0.5 collective-permute-start.7
  27.7 1.3 collective-permute-start.13
  29.0 0.9 collective-permute-start.14
  29.9 1.7 collective-permute-start.10
  31.6 0.7 copy-done.18
  32.3 8.2 %bin_traces.6.refs_0_ = f32[256,4096]{1,0:T(8,128)} custom-call(s32[1]{0:T(128)} %bitcast.2.origin_ref, f32[256,256]{1,0:T(8,128)} %copy.16.matrix_ref, f32[256,4096]{1,0:T(8,128)} %bin_traces.5.refs_0_, f32[72,1024]{1,0:T(8,128)} %copy-done.2, f32[72,1024]{1,0:T(8,128)} %copy-done.18, f32[72,1024]{1,0:T(8,128)} %copy-done.16, ...), custom_call_target="tpu_custom_call" | custom-call | flops 4294967296 | bytes 4194304 | tf_op jit(solution)/shard_map/bin_traces/pallas_call | solution.py:167
  41.2 1.5 collective-permute-done.13
  42.7 1.7 collective-permute-start.15
  44.5 0.7 copy-done.17
  45.2 0.7 copy-done.19
  45.9 8.2 %bin_traces.7.refs_0_ = f32[256,4096]{1,0:T(8,128)} custom-call(s32[1]{0:T(128)} %bitcast.2.origin_ref, f32[256,256]{1,0:T(8,128)} %copy.16.matrix_ref, f32[256,4096]{1,0:T(8,128)} %bin_traces.6.refs_0_, f32[72,1024]{1,0:T(8,128)} %copy-done.3, f32[72,1024]{1,0:T(8,128)} %copy-done.17, f32[72,1024]{1,0:T(8,128)} %copy-done.15, f32[72,1024]{1,0:T(8,128)} %copy-done.19), custom_call_target="tpu_custom_call" | custom-call | flops 4294967296 | bytes 4194304 | tf_op jit(solution)/shard_map/bin_traces/pallas_call | solution.py:167
  54.7 0.6 pad_add_fusion.order_ref
  56.5 0.7 copy-done.12
  57.2 9.6 %bin_traces.8.refs_0_ = bf16[2,256,2048]{2,1,0:T(8,128)(2,1)} custom-call(s32[1]{0:T(128)} %bitcast.2.origin_ref, f32[256,256]{1,0:T(8,128)} %copy.16.matrix_ref, f32[256,4096]{1,0:T(8,128)} %bin_traces.7.refs_0_, f32[72,1024]{1,0:T(8,128)} %copy-done.5, f32[72,1024]{1,0:T(8,128)} %copy-done.11, f32[72,1024]{1,0:T(8,128)} %copy-done.10, f32[72,1024]{1,0:T(8,128)} %copy-done.12), custom_call_target="tpu_custom_call" | custom-call | flops 4294967296 | bytes 4194304 | tf_op jit(solution)/shard_map/bin_traces/pallas_call | solution.py:167
  66.8 18.8 %multiply.3 = (f32[128,2048]{1,0:T(8,128)}, f32[128,2048]{1,0:T(8,128)}) custom-call(s32[2]{0:T(128)} %pad_add_fusion.order_ref, f32[2,2048,2048]{2,1,0:T(8,128)} %a_ref.3, bf16[2,256,2048]{2,1,0:T(8,128)(2,1)} %bin_traces.8.refs_0_), custom_call_target="tpu_custom_call" | custom-call | flops 12884901888 | bytes 33554432 | tf_op jit(solution)/shard_map/multiply/pallas_call | solution.py:233
  85.7 2.7 %collective-permute-done.18 = f32[128,2048]{1,0:T(8,128)S(1)} collective-permute-done((f32[128,2048]{1,0:T(8,128)}, f32[128,2048]{1,0:T(8,128)S(1)}, u32[]{:S(2)}, u32[]{:S(2)}) %collective-permute-start.18) | collective-permute-done | bytes 1048608 | tf_op jit(solution)/shard_map/ppermute | solution.py:44
  88.4 1.3 add.40
  90.6 14.4 %bin_traces.9 = f32[64,2048]{1,0:T(8,128)} custom-call(s32[1]{0:T(128)} %bitcast.6.origin_ref, f32[256,256]{1,0:T(8,128)} %copy.16.matrix_ref, f32[72,1024]{1,0:T(8,128)} %copy-done.4, f32[72,1024]{1,0:T(8,128)} %copy-done.2, f32[72,1024]{1,0:T(8,128)} %copy-done.3, f32[72,1024]{1,0:T(8,128)} %copy-done.5), custom_call_target="tpu_custom_call" | custom-call | flops 4294967296 | bytes 1048576 | tf_op jit(solution)/shard_map/bin_traces/pallas_call | solution.py:167
  105.1 0.9 copy-done
  106.0 0.7 collective-permute-start.20
  106.7 6.2 %collective-permute-start.21 = (f32[64,2048]{1,0:T(8,128)S(1)}, f32[64,2048]{1,0:T(8,128)S(1)}, u32[]{:S(2)}, u32[]{:S(2)}) collective-permute-start(f32[64,2048]{1,0:T(8,128)S(1)} %bitcast_subtract_fusion), channel_id=1, source_target_pairs={{0,4},{1,12},{2,0},{3,8},{4,5},{5,13},{6,1},{7,9},{8,6},{9,14},{10... | collective-permute-start | bytes 1572872 | tf_op jit(solution)/shard_map/ppermute | solution.py:262
  112.9 2.4 %collective-permute-start.22 = (f32[64,2048]{1,0:T(8,128)S(1)}, f32[64,2048]{1,0:T(8,128)S(1)}, u32[]{:S(2)}, u32[]{:S(2)}) collective-permute-start(f32[64,2048]{1,0:T(8,128)S(1)} %bitcast_subtract_fusion), channel_id=1, source_target_pairs={{0,8},{1,0},{2,12},{3,4},{4,9},{5,1},{6,13},{7,5},{8,10},{9,2},{10... | collective-permute-start | bytes 1572872 | tf_op jit(solution)/shard_map/ppermute | solution.py:262
  115.3 2.9 %collective-permute-start.23 = (f32[64,2048]{1,0:T(8,128)S(1)}, f32[64,2048]{1,0:T(8,128)S(1)}, u32[]{:S(2)}, u32[]{:S(2)}) collective-permute-start(f32[64,2048]{1,0:T(8,128)S(1)} %bitcast_subtract_fusion), channel_id=1, source_target_pairs={{0,12},{1,4},{2,8},{3,0},{4,13},{5,5},{6,9},{7,1},{8,14},{9,6},{10... | collective-permute-start | bytes 1572872 | tf_op jit(solution)/shard_map/ppermute | solution.py:262
  118.2 19.4 %collective-permute-done.21.refs_1_ = f32[64,2048]{1,0:T(8,128)S(1)} collective-permute-done((f32[64,2048]{1,0:T(8,128)S(1)}, f32[64,2048]{1,0:T(8,128)S(1)}, u32[]{:S(2)}, u32[]{:S(2)}) %collective-permute-start.21) | collective-permute-done | bytes 524320 | tf_op jit(solution)/shard_map/ppermute | solution.py:262
  137.6 8.9 %collective-permute-done.23.refs_3_ = f32[64,2048]{1,0:T(8,128)S(1)} collective-permute-done((f32[64,2048]{1,0:T(8,128)S(1)}, f32[64,2048]{1,0:T(8,128)S(1)}, u32[]{:S(2)}, u32[]{:S(2)}) %collective-permute-start.23) | collective-permute-done | bytes 524320 | tf_op jit(solution)/shard_map/ppermute | solution.py:262
  146.6 0.8 copy-done.9
  147.4 19.2 %multiply.4 = (f32[128,2048]{1,0:T(8,128)}, f32[128,2048]{1,0:T(8,128)}) custom-call(s32[2]{0:T(128)} %pad_add_fusion.order_ref, f32[2,2048,2048]{2,1,0:T(8,128)} %a_ref.3, f32[64,2048]{1,0:T(8,128)} %copy-done.6, f32[64,2048]{1,0:T(8,128)} %copy-done.7, f32[64,2048]{1,0:T(8,128)} %copy-done.8, f32[64,2048]{1,0:T(8,128)} %copy-done.9), custom_call_target="tpu_custom_call" | custom-call | flops 12884901888 | bytes 33554432 | tf_op jit(solution)/shard_map/multiply/pallas_call | solution.py:233
  166.5 0.9 collective-permute-start.24
  167.4 2.5 %collective-permute-done.24 = f32[128,2048]{1,0:T(8,128)S(1)} collective-permute-done((f32[128,2048]{1,0:T(8,128)}, f32[128,2048]{1,0:T(8,128)S(1)}, u32[]{:S(2)}, u32[]{:S(2)}) %collective-permute-start.24) | collective-permute-done | bytes 1048608 | tf_op jit(solution)/shard_map/ppermute | solution.py:44
  169.9 1.3 add.43
  171.3 14.8 %collective-permute-start.25 = (f32[64,2048]{1,0:T(8,128)S(1)}, f32[64,2048]{1,0:T(8,128)S(1)}, u32[]{:S(2)}, u32[]{:S(2)}) collective-permute-start(f32[64,2048]{1,0:T(8,128)S(1)} %slice.61), channel_id=1, source_target_pairs={{0,2},{1,3},{2,0},{3,1},{4,6},{5,7},{6,4},{7,5},{8,10},{9,11},{10,... | collective-permute-start | bytes 1572872 | tf_op jit(solution)/shard_map/ppermute | solution.py:44
  186.1 12.2 %collective-permute-done.25 = f32[64,2048]{1,0:T(8,128)S(1)} collective-permute-done((f32[64,2048]{1,0:T(8,128)S(1)}, f32[64,2048]{1,0:T(8,128)S(1)}, u32[]{:S(2)}, u32[]{:S(2)}) %collective-permute-start.25) | collective-permute-done | bytes 524320 | tf_op jit(solution)/shard_map/ppermute | solution.py:44
  198.6 1.2 copy.19
  (76 shorter events, 4.8 us)
Async XLA Ops:
  1.8 17.0 %copy-start.4 = (f32[72,1024]{1,0:T(8,128)}, f32[72,1024]{1,0:T(8,128)S(1)}, u32[]{:S(2)}) copy-start(f32[72,1024]{1,0:T(8,128)S(1)} %pad_maximum_fusion.1.refs_0_) | copy-start | bytes 884740
  1.8 10.0 %collective-permute-start = (f32[72,1024]{1,0:T(8,128)S(1)}, f32[72,1024]{1,0:T(8,128)S(1)}, u32[]{:S(2)}, u32[]{:S(2)}) collective-permute-start(f32[72,1024]{1,0:T(8,128)S(1)} %pad_maximum_fusion.1.refs_0_), channel_id=1, source_target_pairs={{0,2},{1,3},{2,0},{3,1},{4,6},{5,7},{6,4},{7,5},{8,10},{9,11},{10,... | collective-permute-start | bytes 884744 | tf_op jit(solution)/shard_map/ppermute | solution.py:44
  4.8 10.3 %collective-permute-start.3 = (f32[72,1024]{1,0:T(8,128)S(1)}, f32[72,1024]{1,0:T(8,128)S(1)}, u32[]{:S(2)}, u32[]{:S(2)}) collective-permute-start(f32[72,1024]{1,0:T(8,128)S(1)} %pad_maximum_fusion.1.refs_0_), channel_id=1, source_target_pairs={{4,0},{8,4},{12,8},{5,1},{9,5},{13,9},{6,2},{10,6},{14,10},{7,3},{... | collective-permute-start | bytes 884744 | tf_op jit(solution)/shard_map/ppermute | solution.py:53
  6.1 10.2 %collective-permute-start.4 = (f32[72,1024]{1,0:T(8,128)S(1)}, f32[72,1024]{1,0:T(8,128)S(1)}, u32[]{:S(2)}, u32[]{:S(2)}) collective-permute-start(f32[72,1024]{1,0:T(8,128)S(1)} %pad_maximum_fusion.1.refs_0_), channel_id=1, source_target_pairs={{0,4},{4,8},{8,12},{1,5},{5,9},{9,13},{2,6},{6,10},{10,14},{3,7},{... | collective-permute-start | bytes 884744 | tf_op jit(solution)/shard_map/ppermute | solution.py:52
  11.8 7.0 %copy-start.13 = (f32[72,1024]{1,0:T(8,128)}, f32[72,1024]{1,0:T(8,128)S(1)}, u32[]{:S(2)}) copy-start(f32[72,1024]{1,0:T(8,128)S(1)} %collective-permute-done.refs_2_) | copy-start | bytes 884740
  11.8 7.0 %collective-permute-start.1 = (f32[72,1024]{1,0:T(8,128)S(1)}, f32[72,1024]{1,0:T(8,128)S(1)}, u32[]{:S(2)}, u32[]{:S(2)}) collective-permute-start(f32[72,1024]{1,0:T(8,128)S(1)} %pad_maximum_fusion.1.refs_0_), channel_id=1, source_target_pairs={{0,1},{1,0},{2,3},{3,2},{4,5},{5,4},{6,7},{7,6},{8,9},{9,8},{10,11... | collective-permute-start | bytes 884744 | tf_op jit(solution)/shard_map/ppermute | solution.py:44
  11.8 7.0 %collective-permute-start.2 = (f32[72,1024]{1,0:T(8,128)S(1)}, f32[72,1024]{1,0:T(8,128)}, u32[]{:S(2)}, u32[]{:S(2)}) collective-permute-start(f32[72,1024]{1,0:T(8,128)S(1)} %collective-permute-done.refs_2_), channel_id=1, source_target_pairs={{0,1},{1,0},{2,3},{3,2},{4,5},{5,4},{6,7},{7,6},{8,9},{9,8},{10,11... | collective-permute-start | bytes 884744 | tf_op jit(solution)/shard_map/ppermute | solution.py:44
  16.4 10.7 %copy-start.2 = (f32[72,1024]{1,0:T(8,128)}, f32[72,1024]{1,0:T(8,128)S(1)}, u32[]{:S(2)}) copy-start(f32[72,1024]{1,0:T(8,128)S(1)} %broadcast_select_fusion.1.refs_1_) | copy-start | bytes 884740
  16.4 11.3 %collective-permute-start.8 = (f32[72,1024]{1,0:T(8,128)S(1)}, f32[72,1024]{1,0:T(8,128)S(1)}, u32[]{:S(2)}, u32[]{:S(2)}) collective-permute-start(f32[72,1024]{1,0:T(8,128)S(1)} %collective-permute-done.3), channel_id=1, source_target_pairs={{4,0},{8,4},{5,1},{9,5},{6,2},{10,6},{7,3},{11,7},{20,16},{24,20},... | collective-permute-start | bytes 884744 | tf_op jit(solution)/shard_map/ppermute | solution.py:53
  17.7 10.0 %collective-permute-start.9 = (f32[72,1024]{1,0:T(8,128)S(1)}, f32[72,1024]{1,0:T(8,128)S(1)}, u32[]{:S(2)}, u32[]{:S(2)}) collective-permute-start(f32[72,1024]{1,0:T(8,128)S(1)} %collective-permute-done.4), channel_id=1, source_target_pairs={{4,8},{8,12},{5,9},{9,13},{6,10},{10,14},{7,11},{11,15},{20,24},{2... | collective-permute-start | bytes 884744 | tf_op jit(solution)/shard_map/ppermute | solution.py:52
  18.4 8.7 %collective-permute-start.5 = (f32[72,1024]{1,0:T(8,128)S(1)}, f32[72,1024]{1,0:T(8,128)S(1)}, u32[]{:S(2)}, u32[]{:S(2)}) collective-permute-start(f32[72,1024]{1,0:T(8,128)S(1)} %broadcast_select_fusion.1.refs_1_), channel_id=1, source_target_pairs={{0,2},{1,3},{2,0},{3,1},{4,6},{5,7},{6,4},{7,5},{8,10},{9,11},{10,... | collective-permute-start | bytes 884744 | tf_op jit(solution)/shard_map/ppermute | solution.py:44
  18.8 0.7 copy-start.14
  27.1 4.5 %copy-start.16 = (f32[72,1024]{1,0:T(8,128)}, f32[72,1024]{1,0:T(8,128)S(1)}, u32[]{:S(2)}) copy-start(f32[72,1024]{1,0:T(8,128)S(1)} %collective-permute-done.5.refs_3_) | copy-start | bytes 884740
  27.1 4.5 %collective-permute-start.6 = (f32[72,1024]{1,0:T(8,128)S(1)}, f32[72,1024]{1,0:T(8,128)S(1)}, u32[]{:S(2)}, u32[]{:S(2)}) collective-permute-start(f32[72,1024]{1,0:T(8,128)S(1)} %broadcast_select_fusion.1.refs_1_), channel_id=1, source_target_pairs={{0,1},{1,0},{2,3},{3,2},{4,5},{5,4},{6,7},{7,6},{8,9},{9,8},{10,11... | collective-permute-start | bytes 884744 | tf_op jit(solution)/shard_map/ppermute | solution.py:44
  27.2 4.4 %collective-permute-start.7 = (f32[72,1024]{1,0:T(8,128)S(1)}, f32[72,1024]{1,0:T(8,128)}, u32[]{:S(2)}, u32[]{:S(2)}) collective-permute-start(f32[72,1024]{1,0:T(8,128)S(1)} %collective-permute-done.5.refs_3_), channel_id=1, source_target_pairs={{0,1},{1,0},{2,3},{3,2},{4,5},{5,4},{6,7},{7,6},{8,9},{9,8},{10,11... | collective-permute-start | bytes 884744 | tf_op jit(solution)/shard_map/ppermute | solution.py:44
  27.7 12.9 %copy-start.3 = (f32[72,1024]{1,0:T(8,128)}, f32[72,1024]{1,0:T(8,128)S(1)}, u32[]{:S(2)}) copy-start(f32[72,1024]{1,0:T(8,128)S(1)} %broadcast_select_fusion.refs_1_.refs_2_) | copy-start | bytes 884740
  27.7 14.9 %collective-permute-start.13 = (f32[72,1024]{1,0:T(8,128)S(1)}, f32[72,1024]{1,0:T(8,128)S(1)}, u32[]{:S(2)}, u32[]{:S(2)}) collective-permute-start(f32[72,1024]{1,0:T(8,128)S(1)} %collective-permute-done.8), channel_id=1, source_target_pairs={{4,0},{5,1},{6,2},{7,3},{20,16},{21,17},{22,18},{23,19}} | collective-permute-start | bytes 884744 | tf_op jit(solution)/shard_map/ppermute | solution.py:53
  29.0 13.6 %collective-permute-start.14 = (f32[72,1024]{1,0:T(8,128)S(1)}, f32[72,1024]{1,0:T(8,128)S(1)}, u32[]{:S(2)}, u32[]{:S(2)}) collective-permute-start(f32[72,1024]{1,0:T(8,128)S(1)} %collective-permute-done.9), channel_id=1, source_target_pairs={{8,12},{9,13},{10,14},{11,15},{24,28},{25,29},{26,30},{27,31}} | collective-permute-start | bytes 884744 | tf_op jit(solution)/shard_map/ppermute | solution.py:52
  29.9 10.7 %collective-permute-start.10 = (f32[72,1024]{1,0:T(8,128)S(1)}, f32[72,1024]{1,0:T(8,128)S(1)}, u32[]{:S(2)}, u32[]{:S(2)}) collective-permute-start(f32[72,1024]{1,0:T(8,128)S(1)} %broadcast_select_fusion.refs_1_.refs_2_), channel_id=1, source_target_pairs={{0,2},{1,3},{2,0},{3,1},{4,6},{5,7},{6,4},{7,5},{8,10},{9,11},{10,... | collective-permute-start | bytes 884744 | tf_op jit(solution)/shard_map/ppermute | solution.py:44
  31.6 0.7 copy-start.18
  40.6 3.9 %copy-start.15 = (f32[72,1024]{1,0:T(8,128)}, f32[72,1024]{1,0:T(8,128)S(1)}, u32[]{:S(2)}) copy-start(f32[72,1024]{1,0:T(8,128)S(1)} %collective-permute-done.10.refs_3_) | copy-start | bytes 884740
  40.6 3.9 %collective-permute-start.11 = (f32[72,1024]{1,0:T(8,128)S(1)}, f32[72,1024]{1,0:T(8,128)S(1)}, u32[]{:S(2)}, u32[]{:S(2)}) collective-permute-start(f32[72,1024]{1,0:T(8,128)S(1)} %broadcast_select_fusion.refs_1_.refs_2_), channel_id=1, source_target_pairs={{0,1},{1,0},{2,3},{3,2},{4,5},{5,4},{6,7},{7,6},{8,9},{9,8},{10,11... | collective-permute-start | bytes 884744 | tf_op jit(solution)/shard_map/ppermute | solution.py:44
  40.7 3.8 %collective-permute-start.12 = (f32[72,1024]{1,0:T(8,128)S(1)}, f32[72,1024]{1,0:T(8,128)S(1)}, u32[]{:S(2)}, u32[]{:S(2)}) collective-permute-start(f32[72,1024]{1,0:T(8,128)S(1)} %collective-permute-done.10.refs_3_), channel_id=1, source_target_pairs={{0,1},{1,0},{2,3},{3,2},{4,5},{5,4},{6,7},{7,6},{8,9},{9,8},{10,11... | collective-permute-start | bytes 884744 | tf_op jit(solution)/shard_map/ppermute | solution.py:44
  42.7 11.4 %copy-start.5 = (f32[72,1024]{1,0:T(8,128)}, f32[72,1024]{1,0:T(8,128)S(1)}, u32[]{:S(2)}) copy-start(f32[72,1024]{1,0:T(8,128)S(1)} %select_select_fusion.refs_1_.refs_3_) | copy-start | bytes 884740
  42.7 11.4 %collective-permute-start.15 = (f32[72,1024]{1,0:T(8,128)S(1)}, f32[72,1024]{1,0:T(8,128)S(1)}, u32[]{:S(2)}, u32[]{:S(2)}) collective-permute-start(f32[72,1024]{1,0:T(8,128)S(1)} %select_select_fusion.refs_1_.refs_3_), channel_id=1, source_target_pairs={{0,2},{1,3},{2,0},{3,1},{4,6},{5,7},{6,4},{7,5},{8,10},{9,11},{10,... | collective-permute-start | bytes 884744 | tf_op jit(solution)/shard_map/ppermute | solution.py:44
  44.4 0.7 copy-start.17
  45.2 0.7 copy-start.19
  54.1 2.1 %copy-start.10 = (f32[72,1024]{1,0:T(8,128)}, f32[72,1024]{1,0:T(8,128)S(1)}, u32[]{:S(2)}) copy-start(f32[72,1024]{1,0:T(8,128)S(1)} %collective-permute-done.15.refs_3_) | copy-start | bytes 884740
  54.1 1.6 collective-permute-start.16
  54.2 2.0 collective-permute-start.17
  55.8 0.7 copy-start.11
  56.5 0.7 copy-start.12
  85.6 4.7 %copy-start.1 = (f32[32,2,2048]{2,1,0:T(2,128)S(1)}, f32[32,2,2048]{2,1,0:T(2,128)}, u32[]{:S(2)}) copy-start(f32[32,2,2048]{2,1,0:T(2,128)} %param.13) | copy-start | bytes 1572868
  85.6 2.9 %collective-permute-start.18 = (f32[128,2048]{1,0:T(8,128)}, f32[128,2048]{1,0:T(8,128)S(1)}, u32[]{:S(2)}, u32[]{:S(2)}) collective-permute-start(f32[128,2048]{1,0:T(8,128)} %get-tuple-element.67), channel_id=1, source_target_pairs={{0,1},{1,0},{2,3},{3,2},{4,5},{5,4},{6,7},{7,6},{8,9},{9,8},{10,11... | collective-permute-start | bytes 3145736 | tf_op jit(solution)/shard_map/ppermute | solution.py:44
  89.8 15.1 %collective-permute-start.19 = (f32[64,2048]{1,0:T(8,128)S(1)}, f32[64,2048]{1,0:T(8,128)S(1)}, u32[]{:S(2)}, u32[]{:S(2)}) collective-permute-start(f32[64,2048]{1,0:T(8,128)S(1)} %slice.56), channel_id=1, source_target_pairs={{0,2},{1,3},{2,0},{3,1},{4,6},{5,7},{6,4},{7,5},{8,10},{9,11},{10,... | collective-permute-start | bytes 1572872 | tf_op jit(solution)/shard_map/ppermute | solution.py:44
  104.9 1.0 copy-start
  106.0 12.2 %collective-permute-start.20 = (f32[64,2048]{1,0:T(8,128)S(1)}, f32[64,2048]{1,0:T(8,128)S(1)}, u32[]{:S(2)}, u32[]{:S(2)}) collective-permute-start(f32[64,2048]{1,0:T(8,128)S(1)} %bitcast_subtract_fusion), channel_id=1, source_target_pairs={{0,0},{1,8},{2,4},{3,12},{4,1},{5,9},{6,5},{7,13},{8,2},{9,10},{10... | collective-permute-start | bytes 1572872 | tf_op jit(solution)/shard_map/ppermute | solution.py:262
  106.7 30.9 %collective-permute-start.21 = (f32[64,2048]{1,0:T(8,128)S(1)}, f32[64,2048]{1,0:T(8,128)S(1)}, u32[]{:S(2)}, u32[]{:S(2)}) collective-permute-start(f32[64,2048]{1,0:T(8,128)S(1)} %bitcast_subtract_fusion), channel_id=1, source_target_pairs={{0,4},{1,12},{2,0},{3,8},{4,5},{5,13},{6,1},{7,9},{8,6},{9,14},{10... | collective-permute-start | bytes 1572872 | tf_op jit(solution)/shard_map/ppermute | solution.py:262
  112.9 24.7 %collective-permute-start.22 = (f32[64,2048]{1,0:T(8,128)S(1)}, f32[64,2048]{1,0:T(8,128)S(1)}, u32[]{:S(2)}, u32[]{:S(2)}) collective-permute-start(f32[64,2048]{1,0:T(8,128)S(1)} %bitcast_subtract_fusion), channel_id=1, source_target_pairs={{0,8},{1,0},{2,12},{3,4},{4,9},{5,1},{6,13},{7,5},{8,10},{9,2},{10... | collective-permute-start | bytes 1572872 | tf_op jit(solution)/shard_map/ppermute | solution.py:262
  115.3 31.2 %collective-permute-start.23 = (f32[64,2048]{1,0:T(8,128)S(1)}, f32[64,2048]{1,0:T(8,128)S(1)}, u32[]{:S(2)}, u32[]{:S(2)}) collective-permute-start(f32[64,2048]{1,0:T(8,128)S(1)} %bitcast_subtract_fusion), channel_id=1, source_target_pairs={{0,12},{1,4},{2,8},{3,0},{4,13},{5,5},{6,9},{7,1},{8,14},{9,6},{10... | collective-permute-start | bytes 1572872 | tf_op jit(solution)/shard_map/ppermute | solution.py:262
  118.2 28.3 %copy-start.6 = (f32[64,2048]{1,0:T(8,128)}, f32[64,2048]{1,0:T(8,128)S(1)}, u32[]{:S(2)}) copy-start(f32[64,2048]{1,0:T(8,128)S(1)} %collective-permute-done.20.refs_0_) | copy-start | bytes 1572868
  137.6 8.9 %copy-start.7 = (f32[64,2048]{1,0:T(8,128)}, f32[64,2048]{1,0:T(8,128)S(1)}, u32[]{:S(2)}) copy-start(f32[64,2048]{1,0:T(8,128)S(1)} %collective-permute-done.21.refs_1_) | copy-start | bytes 1572868
  137.6 8.9 %copy-start.8 = (f32[64,2048]{1,0:T(8,128)}, f32[64,2048]{1,0:T(8,128)S(1)}, u32[]{:S(2)}) copy-start(f32[64,2048]{1,0:T(8,128)S(1)} %collective-permute-done.22.refs_2_) | copy-start | bytes 1572868
  146.5 0.8 copy-start.9
  166.5 3.4 %collective-permute-start.24 = (f32[128,2048]{1,0:T(8,128)}, f32[128,2048]{1,0:T(8,128)S(1)}, u32[]{:S(2)}, u32[]{:S(2)}) collective-permute-start(f32[128,2048]{1,0:T(8,128)} %get-tuple-element.70), channel_id=1, source_target_pairs={{0,1},{1,0},{2,3},{3,2},{4,5},{5,4},{6,7},{7,6},{8,9},{9,8},{10,11... | collective-permute-start | bytes 3145736 | tf_op jit(solution)/shard_map/ppermute | solution.py:44
  171.3 27.0 %collective-permute-start.25 = (f32[64,2048]{1,0:T(8,128)S(1)}, f32[64,2048]{1,0:T(8,128)S(1)}, u32[]{:S(2)}, u32[]{:S(2)}) collective-permute-start(f32[64,2048]{1,0:T(8,128)S(1)} %slice.61), channel_id=1, source_target_pairs={{0,2},{1,3},{2,0},{3,1},{4,6},{5,7},{6,4},{7,5},{8,10},{9,11},{10,... | collective-permute-start | bytes 1572872 | tf_op jit(solution)/shard_map/ppermute | solution.py:44
